TPU v7x, 32 devices: a whole 2x2x4 slice. The times are simulated.
32 devices in a mesh: groups: 2 (over y), blk: 16 (over z, x, core).
Axes of the slice: x: 2, y: 2, z: 4, core: 2. Of those that a mesh axis runs over, the one named last changes fastest.
Arguments:
- queries: bfloat16 [16384, 2048], P(('groups', 'blk')), parts along dimension 0, may hold values from -6 to 6
- gallery: bfloat16 [49152, 2048], P(('groups', 'blk')), parts along dimension 0, may hold values from -6 to 6
- neighbors: int32 [16384, 4, 8], P(('groups', 'blk')), parts along dimension 0, may hold values from 0 to 1535
- counts: int32 [32], P(('groups', 'blk')), parts along dimension 0, may hold values from 768 to 1536, as said below
Outputs:
- expanded: bfloat16 [16384, 2048], P(('groups', 'blk')), parts along dimension 0
There are 2 independent parts, one for each index of `groups`. A program takes and returns all parts, laid end to end along the dimension named above; each array names one. Nothing has to cross between parts.
Inputs may be any that keep to these rules, and one draw needn't show every extreme that they name: `counts`: the largest count equals 1536 in every draw.
All inputs are finite; a program needn't handle non-finite values.
Results may differ from a plain program's by a relative error of at most 0.0085.
Values may be sent and summed in bfloat16 or wider, within the bound.
No kernel may reach another device: no remote copies, remote signals or barrier semaphores. Data moves between devices by JAX's collectives and lax.ppermute only.
A program may use at most 192 MiB of HBM per device.

v0:
```python
import jax
import jax.numpy as jnp
from jax import lax
from jax.sharding import PartitionSpec as P

STEPS = 4


def passed_along(block, axis, distance):
    devices = range(lax.axis_size(axis))
    route = [((i - distance) % len(devices), i) for i in devices]
    return lax.ppermute(block, axis, route)


def contribution(query_rows, picks, gallery, live):
    scale = 1.0 / gallery.shape[1] ** 0.5
    width = picks.shape[1]
    rows = gallery[picks]
    score = jnp.einsum("qd,qkd->qk", query_rows, rows, preferred_element_type=jnp.float32) * scale
    relu_s = jnp.maximum(score, 0.0)
    weight = relu_s * relu_s * relu_s * (picks < live).astype(jnp.float32)
    earlier = lax.broadcasted_iota(jnp.int32, (width, width), 1) < lax.broadcasted_iota(
        jnp.int32, (width, width), 0
    )
    same = picks[:, :, None] == picks[:, None, :]
    summed = jnp.sum(jnp.where(same, weight[:, None, :], 0.0), axis=2)
    repeat = jnp.any(same & earlier[None, :, :], axis=2)
    weight_b = jnp.where(repeat, 0.0, summed).astype(jnp.bfloat16)
    total = jnp.einsum("qk,qkd->qd", weight_b, rows, preferred_element_type=jnp.float32)
    mass = jnp.sum(weight, axis=1)
    return (total, mass)


def finish(query_rows, total, mass):
    return ((query_rows.astype(jnp.float32) + total) / (1.0 + mass)[:, None]).astype(jnp.bfloat16)


def on_device(queries, gallery, neighbors, counts):
    live = counts[0]
    query_now = queries
    index_now = neighbors
    total = jnp.zeros(queries.shape, jnp.float32)
    mass = jnp.zeros((queries.shape[0],), jnp.float32)
    for step in range(STEPS):
        part_total, part_mass = contribution(query_now, index_now[:, step, :], gallery, live)
        total = total + part_total
        mass = mass + part_mass
        if step + 1 < STEPS:
            query_now = passed_along(query_now, "blk", 1)
            index_now = passed_along(index_now, "blk", 1)
            total, mass = passed_along((total, mass), "blk", 1)
    done = finish(query_now, total, mass)
    return passed_along(done, "blk", 1 - STEPS)


def solution(mesh):
    return jax.shard_map(
        on_device,
        mesh=mesh,
        in_specs=(
            P(("groups", "blk"), None),
            P(("groups", "blk"), None),
            P(("groups", "blk"), None, None),
            P(("groups", "blk")),
        ),
        out_specs=P(("groups", "blk"), None),
        check_vma=False,
    )
```

profile of v0, /device:TPU:1, one launch (start us, length us, event | category | flops | bytes accessed | tf_op | source)
XLA Modules:
  0.0 397.0 jit_solution(6617545060125359988)
XLA Ops:
  0.0 2.6 collective-permute-start.4
  2.6 0.7 compare_select_fusion.7
  3.7 34.9 %gather_fusion = bf16[4096,2048]{1,0:T(8,128)(2,1)} fusion(bf16[1536,2048]{1,0:T(8,128)(2,1)} %param.5, s32[4096]{0:T(1024)S(1)} %broadcast_clamp_fusion.3), kind=kCustom, calls=%fused_computation | custom fusion | bytes 33570816 | tf_op jit(solution)/shard_map/gather | solution.py:18
  38.6 12.4 %fusion.12 = f32[512,1,8]{2,1,0:T(1,128)S(1)} fusion(bf16[4096,2048]{1,0:T(8,128)(2,1)} %gather_fusion, bf16[512,2048,1]{1,0,2:T(8,128)(2,1)} %bitcast.121), kind=kOutput, calls=%fused_computation.16 | convolution fusion | flops 16777216 | bytes 18890752 | tf_op jit(solution)/shard_map/qd,qkd->qk/dot_general | solution.py:19
  51.7 0.6 fusion.49
  52.7 1.7 collective-permute-start.6
  54.4 34.9 %gather_fusion.1 = bf16[4096,2048]{1,0:T(8,128)(2,1)} fusion(bf16[1536,2048]{1,0:T(8,128)(2,1)} %param.5, s32[4096]{0:T(1024)S(1)} %broadcast_clamp_fusion.2), kind=kCustom, calls=%fused_computation.1 | custom fusion | bytes 33570816 | tf_op jit(solution)/shard_map/gather | solution.py:18
  89.4 1.3 collective-permute-done.8
  90.9 12.3 %fusion.8 = f32[512,1,8]{2,1,0:T(1,128)S(1)} fusion(bf16[4096,2048]{1,0:T(8,128)(2,1)} %gather_fusion.1, bf16[512,2048,1]{1,0,2:T(8,128)(2,1)} %bitcast.11), kind=kOutput, calls=%fused_computation.12 | convolution fusion | flops 16777216 | bytes 18890752 | tf_op jit(solution)/shard_map/qd,qkd->qk/dot_general | solution.py:19
  103.7 8.4 %fusion.14 = f32[512,1,2048]{2,1,0:T(1,128)S(1)} fusion(bf16[512,8,1]{1,2,0:T(2,128)(2,1)S(1)} %copy.39, bf16[4096,2048]{1,0:T(8,128)(2,1)} %gather_fusion), kind=kOutput, calls=%fused_computation.18 | convolution fusion | flops 16777216 | bytes 20979712 | tf_op jit(solution)/shard_map/qk,qkd->qd/dot_general | solution.py:29
  112.1 3.9 copy.65
  116.0 2.4 collective-permute-start.3
  118.7 34.9 %gather_fusion.2 = bf16[4096,2048]{1,0:T(8,128)(2,1)} fusion(bf16[1536,2048]{1,0:T(8,128)(2,1)} %param.5, s32[4096]{0:T(1024)S(1)} %broadcast_clamp_fusion.1), kind=kCustom, calls=%fused_computation.2 | custom fusion | bytes 33570816 | tf_op jit(solution)/shard_map/gather | solution.py:18
  153.9 34.9 %gather_fusion.3 = bf16[4096,2048]{1,0:T(8,128)(2,1)} fusion(bf16[1536,2048]{1,0:T(8,128)(2,1)} %param.5, s32[4096]{0:T(1024)S(1)} %broadcast_clamp_fusion), kind=kCustom, calls=%fused_computation.3 | custom fusion | bytes 33570816 | tf_op jit(solution)/shard_map/gather | solution.py:18
  189.0 10.5 %fusion.10 = f32[512,1,2048]{2,1,0:T(1,128)} fusion(bf16[512,8,1]{1,2,0:T(2,128)(2,1)S(1)} %copy.43, bf16[4096,2048]{1,0:T(8,128)(2,1)} %gather_fusion.1), kind=kOutput, calls=%fused_computation.14 | convolution fusion | flops 16777216 | bytes 20979712 | tf_op jit(solution)/shard_map/qk,qkd->qd/dot_general | solution.py:29
  199.5 2.5 collective-permute-start.2
  202.0 12.3 %fusion.4 = f32[512,1,8]{2,1,0:T(1,128)S(1)} fusion(bf16[4096,2048]{1,0:T(8,128)(2,1)} %gather_fusion.2, bf16[512,2048,1]{1,0,2:T(8,128)(2,1)} %bitcast.18), kind=kOutput, calls=%fused_computation.8 | convolution fusion | flops 16777216 | bytes 18890752 | tf_op jit(solution)/shard_map/qd,qkd->qk/dot_general | solution.py:19
  214.5 7.8 %bitcast_add_fusion.2 = f32[512,2048]{1,0:T(8,128)} fusion(f32[512,2048]{1,0:T(8,128)} %collective-permute-done.3, f32[512,1,2048]{2,1,0:T(1,128)} %fusion.10), kind=kLoop, calls=%fused_computation.25 | loop fusion | flops 1048576 | bytes 12582912 | tf_op jit(solution)/shard_map/add | solution.py:46
  222.4 2.9 collective-permute-done.2
  225.3 10.2 %fusion = f32[512,1,8]{2,1,0:T(1,128)S(1)} fusion(bf16[4096,2048]{1,0:T(8,128)(2,1)} %gather_fusion.3, bf16[512,2048,1]{1,0,2:T(8,128)(2,1)S(1)} %bitcast.120), kind=kOutput, calls=%fused_computation.4 | convolution fusion | flops 16777216 | bytes 18890752 | tf_op jit(solution)/shard_map/qd,qkd->qk/dot_general | solution.py:19
  235.9 8.4 %fusion.6 = f32[512,1,2048]{2,1,0:T(1,128)S(1)} fusion(bf16[512,8,1]{1,2,0:T(2,128)(2,1)S(1)} %copy.47, bf16[4096,2048]{1,0:T(8,128)(2,1)} %gather_fusion.2), kind=kOutput, calls=%fused_computation.10 | convolution fusion | flops 16777216 | bytes 20979712 | tf_op jit(solution)/shard_map/qk,qkd->qd/dot_general | solution.py:29
  244.3 25.9 %collective-permute-done.5 = f32[512,2048]{1,0:T(8,128)} collective-permute-done((f32[512,2048]{1,0:T(8,128)}, f32[512,2048]{1,0:T(8,128)}, u32[]{:S(2)}, u32[]{:S(2)}) %collective-permute-start.5) | collective-permute-done | bytes 4194336 | tf_op jit(solution)/shard_map/ppermute | solution.py:12
  270.2 6.4 %bitcast_add_fusion.1 = f32[512,2048]{1,0:T(8,128)} fusion(f32[512,2048]{1,0:T(8,128)} %collective-permute-done.5, f32[512,1,2048]{2,1,0:T(1,128)S(1)} %fusion.6), kind=kLoop, calls=%fused_computation.24 | loop fusion | flops 1048576 | bytes 12582912 | tf_op jit(solution)/shard_map/add | solution.py:46
  276.6 2.5 collective-permute-start.7
  279.1 45.7 %collective-permute-done.9 = f32[512]{0:T(512)S(1)} collective-permute-done((f32[512]{0:T(512)S(1)}, f32[512]{0:T(512)S(1)}, u32[]{:S(2)}, u32[]{:S(2)}) %collective-permute-start.9) | collective-permute-done | bytes 2080 | tf_op jit(solution)/shard_map/ppermute | solution.py:12
  324.9 2.5 collective-permute-start.10
  327.4 5.1 %collective-permute-done.10 = f32[512]{0:T(512)S(1)} collective-permute-done((f32[512]{0:T(512)S(1)}, f32[512]{0:T(512)S(1)}, u32[]{:S(2)}, u32[]{:S(2)}) %collective-permute-start.10) | collective-permute-done | bytes 2080 | tf_op jit(solution)/shard_map/ppermute | solution.py:12
  332.7 5.5 %collective-permute-done.11 = f32[512]{0:T(512)S(1)} collective-permute-done((f32[512]{0:T(512)S(1)}, f32[512]{0:T(512)S(1)}, u32[]{:S(2)}, u32[]{:S(2)}) %collective-permute-start.11) | collective-permute-done | bytes 2080 | tf_op jit(solution)/shard_map/ppermute | solution.py:12
  338.2 8.4 %fusion.2 = f32[512,1,2048]{2,1,0:T(1,128)S(1)} fusion(bf16[512,8,1]{1,2,0:T(2,128)(2,1)S(1)} %copy.51, bf16[4096,2048]{1,0:T(8,128)(2,1)} %gather_fusion.3), kind=kOutput, calls=%fused_computation.6 | convolution fusion | flops 16777216 | bytes 20979712 | tf_op jit(solution)/shard_map/qk,qkd->qd/dot_general | solution.py:29
  346.6 4.6 %fusion.18 = bf16[512,2048]{1,0:T(8,128)(2,1)S(1)} fusion(f32[512,2048]{1,0:T(8,128)} %collective-permute-done.7, f32[512,1,2048]{2,1,0:T(1,128)S(1)} %fusion.2, bf16[512,2048]{1,0:T(8,128)(2,1)S(1)} %collective-permute-done.2, f32[512]{0:T(512)S(1)} %add_add_fusion), kind=kLoop, calls=%fused_computation.23 | loop fusion | flops 5242880 | bytes 12584960 | tf_op jit(solution)/shard_map/convert_element_type | solution.py:35
  351.3 44.4 %collective-permute-done.12 = bf16[512,2048]{1,0:T(8,128)(2,1)S(1)} collective-permute-done((bf16[512,2048]{1,0:T(8,128)(2,1)S(1)}, bf16[512,2048]{1,0:T(8,128)(2,1)S(1)}, u32[]{:S(2)}, u32[]{:S(2)}) %collective-permute-start.12) | collective-permute-done | bytes 2097184 | tf_op jit(solution)/shard_map/ppermute | solution.py:12
  395.6 1.3 copy.68
  (58 shorter events, 3.0 us)
Async XLA Ops:
  0.0 52.4 %collective-permute-start.4 = (s32[512,4,8]{0,2,1:T(8,128)}, s32[512,4,8]{0,2,1:T(8,128)S(1)}, u32[]{:S(2)}, u32[]{:S(2)}) collective-permute-start(s32[512,4,8]{0,2,1:T(8,128)} %param.6), channel_id=1, source_target_pairs={{15,0},{0,1},{1,2},{2,3},{3,4},{4,5},{5,6},{6,7},{7,8},{8,9},{9,10... | collective-permute-start | bytes 196616 | tf_op jit(solution)/shard_map/ppermute | solution.py:12
  2.6 88.3 %collective-permute-start = (bf16[512,2048]{1,0:T(8,128)(2,1)}, bf16[512,2048]{1,0:T(8,128)(2,1)}, u32[]{:S(2)}, u32[]{:S(2)}) collective-permute-start(bf16[512,2048]{1,0:T(8,128)(2,1)} %param.4), channel_id=1, source_target_pairs={{15,0},{0,1},{1,2},{2,3},{3,4},{4,5},{5,6},{6,7},{7,8},{8,9},{9,10... | collective-permute-start | bytes 6291464 | tf_op jit(solution)/shard_map/ppermute | solution.py:12
  38.6 13.1 %copy-start = (s32[512,4,8]{0,2,1:T(8,128)S(1)}, s32[512,4,8]{0,2,1:T(8,128)}, u32[]{:S(2)}) copy-start(s32[512,4,8]{0,2,1:T(8,128)} %param.6) | copy-start | bytes 196612
  52.7 36.6 %collective-permute-start.6 = (s32[512,4,8]{0,2,1:T(8,128)S(1)}, s32[512,4,8]{0,2,1:T(8,128)S(1)}, u32[]{:S(2)}, u32[]{:S(2)}) collective-permute-start(s32[512,4,8]{0,2,1:T(8,128)S(1)} %collective-permute-done.4), channel_id=1, source_target_pairs={{15,0},{0,1},{1,2},{2,3},{3,4},{4,5},{5,6},{6,7},{7,8},{8,9},{9,10... | collective-permute-start | bytes 196616 | tf_op jit(solution)/shard_map/ppermute | solution.py:12
  89.3 1.4 collective-permute-start.8
  116.0 98.5 %collective-permute-start.3 = (f32[512,2048]{1,0:T(8,128)}, f32[512,2048]{1,0:T(8,128)}, u32[]{:S(2)}, u32[]{:S(2)}) collective-permute-start(f32[512,2048]{1,0:T(8,128)} %bitcast.115), channel_id=1, source_target_pairs={{15,0},{0,1},{1,2},{2,3},{3,4},{4,5},{5,6},{6,7},{7,8},{8,9},{9,10... | collective-permute-start | bytes 12582920 | tf_op jit(solution)/shard_map/ppermute | solution.py:12
  118.4 81.2 %collective-permute-start.1 = (bf16[512,2048]{1,0:T(8,128)(2,1)}, bf16[512,2048]{1,0:T(8,128)(2,1)}, u32[]{:S(2)}, u32[]{:S(2)}) collective-permute-start(bf16[512,2048]{1,0:T(8,128)(2,1)} %collective-permute-done), channel_id=1, source_target_pairs={{15,0},{0,1},{1,2},{2,3},{3,4},{4,5},{5,6},{6,7},{7,8},{8,9},{9,10... | collective-permute-start | bytes 6291464 | tf_op jit(solution)/shard_map/ppermute | solution.py:12
  199.5 25.8 %collective-permute-start.2 = (bf16[512,2048]{1,0:T(8,128)(2,1)}, bf16[512,2048]{1,0:T(8,128)(2,1)S(1)}, u32[]{:S(2)}, u32[]{:S(2)}) collective-permute-start(bf16[512,2048]{1,0:T(8,128)(2,1)} %collective-permute-done.1), channel_id=1, source_target_pairs={{15,0},{0,1},{1,2},{2,3},{3,4},{4,5},{5,6},{6,7},{7,8},{8,9},{9,10... | collective-permute-start | bytes 6291464 | tf_op jit(solution)/shard_map/ppermute | solution.py:12
  222.2 48.0 %collective-permute-start.5 = (f32[512,2048]{1,0:T(8,128)}, f32[512,2048]{1,0:T(8,128)}, u32[]{:S(2)}, u32[]{:S(2)}) collective-permute-start(f32[512,2048]{1,0:T(8,128)} %bitcast_add_fusion.2), channel_id=1, source_target_pairs={{15,0},{0,1},{1,2},{2,3},{3,4},{4,5},{5,6},{6,7},{7,8},{8,9},{9,10... | collective-permute-start | bytes 12582920 | tf_op jit(solution)/shard_map/ppermute | solution.py:12
  244.3 34.8 %copy-start.1 = (f32[512]{0:T(512)S(1)}, f32[512]{0:T(512)}, u32[]{:S(2)}) copy-start(f32[512]{0:T(512)} %get-tuple-element.15) | copy-start | bytes 6148
  276.6 70.0 %collective-permute-start.7 = (f32[512,2048]{1,0:T(8,128)}, f32[512,2048]{1,0:T(8,128)}, u32[]{:S(2)}, u32[]{:S(2)}) collective-permute-start(f32[512,2048]{1,0:T(8,128)} %bitcast_add_fusion.1), channel_id=1, source_target_pairs={{15,0},{0,1},{1,2},{2,3},{3,4},{4,5},{5,6},{6,7},{7,8},{8,9},{9,10... | collective-permute-start | bytes 12582920 | tf_op jit(solution)/shard_map/ppermute | solution.py:12
  279.1 45.8 %collective-permute-start.9 = (f32[512]{0:T(512)S(1)}, f32[512]{0:T(512)S(1)}, u32[]{:S(2)}, u32[]{:S(2)}) collective-permute-start(f32[512]{0:T(512)S(1)} %copy-done.1), channel_id=1, source_target_pairs={{15,0},{0,1},{1,2},{2,3},{3,4},{4,5},{5,6},{6,7},{7,8},{8,9},{9,10... | collective-permute-start | bytes 6152 | tf_op jit(solution)/shard_map/ppermute | solution.py:12
  324.9 7.6 %collective-permute-start.10 = (f32[512]{0:T(512)S(1)}, f32[512]{0:T(512)S(1)}, u32[]{:S(2)}, u32[]{:S(2)}) collective-permute-start(f32[512]{0:T(512)S(1)} %add.75), channel_id=1, source_target_pairs={{15,0},{0,1},{1,2},{2,3},{3,4},{4,5},{5,6},{6,7},{7,8},{8,9},{9,10... | collective-permute-start | bytes 6152 | tf_op jit(solution)/shard_map/ppermute | solution.py:12
  332.5 5.7 %collective-permute-start.11 = (f32[512]{0:T(512)S(1)}, f32[512]{0:T(512)S(1)}, u32[]{:S(2)}, u32[]{:S(2)}) collective-permute-start(f32[512]{0:T(512)S(1)} %add.76), channel_id=1, source_target_pairs={{15,0},{0,1},{1,2},{2,3},{3,4},{4,5},{5,6},{6,7},{7,8},{8,9},{9,10... | collective-permute-start | bytes 6152 | tf_op jit(solution)/shard_map/ppermute | solution.py:12
  351.2 44.4 %collective-permute-start.12 = (bf16[512,2048]{1,0:T(8,128)(2,1)S(1)}, bf16[512,2048]{1,0:T(8,128)(2,1)S(1)}, u32[]{:S(2)}, u32[]{:S(2)}) collective-permute-start(bf16[512,2048]{1,0:T(8,128)(2,1)S(1)} %fusion.18), channel_id=1, source_target_pairs={{3,0},{4,1},{5,2},{6,3},{7,4},{8,5},{9,6},{10,7},{11,8},{12,9},{13... | collective-permute-start | bytes 6291464 | tf_op jit(solution)/shard_map/ppermute | solution.py:12
where the time goes:
time: 399 us; the launch traced here: 397 us
  local copies, waits for them, and re-layouts  147 us (37%)
  waiting for transfers between devices  131 us (33%)
  matrix products  83 us (21%)
  other arithmetic  20.7 us (5%)
  starting transfers between devices  14.3 us (4%)
    gather x4, local copies, waits for them, and re-layouts, contribution(): rows = gallery[picks]  140 us
    ppermute x13, waiting for transfers between devices, passed_along(): return lax.ppermute(block, axis, route)  131 us
    dot_general x4, matrix products, contribution(): jnp.einsum('qd,qkd->qk', query_rows, rows, preferred_element_type=jnp.flo...  47.2 us
    dot_general x4, matrix products, contribution(): jnp.einsum('qk,qkd->qd', weight_b, rows, preferred_element_type=jnp.float32)  35.8 us
    ppermute x13, starting transfers between devices, passed_along(): return lax.ppermute(block, axis, route)  14.3 us
    add x2, other arithmetic, on_device(): total = total + part_total  14.2 us
  transfers between devices with their start and end apart: 13, of which 7 were waited for; matrix products, arithmetic and copies ran while one was open for 54% of the time, Pallas kernels for 0%

commit v1 on v0

v1 whole, which is shorter than its diff:
```python
import functools

import jax
import jax.numpy as jnp
from jax import lax
from jax.experimental import pallas as pl
from jax.experimental.pallas import tpu as pltpu
from jax.sharding import PartitionSpec as P

CHUNKS = 2
TILE = 256
NO_PICK = 4095


def meet_kernel(n_gal, topk, scale3, live_ref, q_ref, enc_ref, *refs):
    gal_refs = refs[:n_gal]
    out_ref, mass_ref, w_ref = refs[n_gal:]
    rows = q_ref.shape[0]
    gal_rows, width = gal_refs[0].shape
    q = q_ref[...]
    mass = jnp.zeros((rows, 128), jnp.float32)
    for g in range(n_gal):
        live = live_ref[g]
        enc = enc_ref[:, g * topk : (g + 1) * topk]
        pick = enc & NO_PICK
        pick = jnp.where(pick < live, pick, -1)
        gain = (enc >> 12).astype(jnp.float32) * scale3
        for t in range(gal_rows // TILE):
            tile = gal_refs[g][t * TILE : (t + 1) * TILE, :]
            s = lax.dot_general(q, tile, (((1,), (1,)), ((), ())), preferred_element_type=jnp.float32)
            col = lax.broadcasted_iota(jnp.int32, (rows, TILE), 1) + t * TILE
            c = jnp.zeros((rows, TILE), jnp.float32)
            for k in range(topk):
                c = jnp.where(col == pick[:, k : k + 1], gain[:, k : k + 1], c)
            r = jnp.maximum(s, 0.0)
            w = r * r * (r * c)
            for j in range(TILE // 128):
                mass = mass + w[:, j * 128 : (j + 1) * 128]
            w_ref[g, :, t * TILE : (t + 1) * TILE] = w.astype(jnp.bfloat16)
    mass_ref[...] = jnp.sum(mass, axis=1, keepdims=True)
    for n in range(width // TILE):
        cut = slice(n * TILE, (n + 1) * TILE)
        total = jnp.dot(w_ref[0], gal_refs[0][:, cut], preferred_element_type=jnp.float32)
        for g in range(1, n_gal):
            total = total + jnp.dot(w_ref[g], gal_refs[g][:, cut], preferred_element_type=jnp.float32)
        out_ref[:, cut] = total.astype(out_ref.dtype)


def meet(q, enc, lives, gals, topk, row_block=256):
    rows, width = q.shape
    gal_rows = gals[0].shape[0]
    n_gal = len(gals)
    row_block = min(row_block, rows)
    vmem = pltpu.VMEM
    return pl.pallas_call(
        functools.partial(meet_kernel, n_gal, topk, float(width) ** -1.5),
        grid=(rows // row_block,),
        out_shape=(
            jax.ShapeDtypeStruct((rows, width), jnp.bfloat16),
            jax.ShapeDtypeStruct((rows, 1), jnp.float32),
        ),
        in_specs=[
            pl.BlockSpec(memory_space=pltpu.SMEM),
            pl.BlockSpec((row_block, width), lambda i: (i, 0)),
            pl.BlockSpec((row_block, n_gal * topk), lambda i: (i, 0)),
        ]
        + [pl.BlockSpec((gal_rows, width), lambda i: (0, 0))] * n_gal,
        out_specs=(
            pl.BlockSpec((row_block, width), lambda i: (i, 0)),
            pl.BlockSpec((row_block, 1), lambda i: (i, 0)),
        ),
        scratch_shapes=[vmem((n_gal, row_block, gal_rows), jnp.bfloat16)],
        compiler_params=pltpu.CompilerParams(vmem_limit_bytes=56 * 1024 * 1024),
        cost_estimate=pl.CostEstimate(
            flops=4 * rows * gal_rows * width * n_gal,
            bytes_accessed=2 * n_gal * gal_rows * width + 4 * rows * width,
            transcendentals=0,
        ),
    )(lives, q, enc, *gals)


def on_device(queries, gallery, neighbors, counts):
    n = lax.axis_size("blk")
    core = lax.axis_index("blk") % 2
    rows, width = queries.shape
    topk = neighbors.shape[2]

    def shift(k):
        return [(i, (i + k) % n) for i in range(n)]

    def odd_shift(k):
        return [(i, (i + k) % n if i % 2 else i) for i in range(n)]

    swap = [(i, i ^ 1) for i in range(n)]

    same = neighbors[:, :, :, None] == neighbors[:, :, None, :]
    many = jnp.sum(same.astype(jnp.int32), axis=3)
    order = jnp.arange(topk)
    repeat = jnp.any(same & (order[None, :] < order[:, None]), axis=3)
    enc = jnp.where(repeat, NO_PICK, neighbors + (many << 12))
    enc_own = enc[:, 0]
    enc_near = jnp.concatenate([enc[:, 2], jnp.where(core == 0, enc[:, 3], enc[:, 1])], axis=1)
    enc_far = jnp.where(core == 0, enc[:, 1], enc[:, 3])

    size = rows // CHUNKS
    near = [lax.ppermute(queries[c * size : (c + 1) * size], "blk", shift(2)) for c in range(CHUNKS)]
    enc_near = lax.ppermute(enc_near.T, "blk", shift(2)).T
    enc_far = lax.ppermute(enc_far.T, "blk", odd_shift(4)).T
    far = lax.ppermute(queries, "blk", odd_shift(4))
    other = lax.ppermute(gallery, "blk", swap)
    live = jnp.concatenate([counts, lax.ppermute(counts, "blk", swap)])

    total_own, mass_own = meet(queries, enc_own, live[:1], (gallery,), topk)
    total_far, mass_far = meet(far, enc_far, live[1:], (other,), topk)
    total_far = lax.ppermute(total_far, "blk", odd_shift(-4))
    mass_far = lax.ppermute(mass_far[:, 0], "blk", odd_shift(-4))
    outs = []
    for c in range(CHUNKS):
        cut = slice(c * size, (c + 1) * size)
        total, mass = meet(near[c], enc_near[cut], live, (gallery, other), topk)
        total = lax.ppermute(total, "blk", shift(-2))
        mass = lax.ppermute(mass[:, 0], "blk", shift(-2))
        mass = mass + mass_own[cut, 0] + mass_far[cut]
        sums = queries[cut].astype(jnp.float32) + total_own[cut] + total_far[cut] + total
        outs.append((sums / (1.0 + mass)[:, None]).astype(jnp.bfloat16))
    return jnp.concatenate(outs, axis=0)


def solution(mesh):
    return jax.shard_map(
        on_device,
        mesh=mesh,
        in_specs=(
            P(("groups", "blk"), None),
            P(("groups", "blk"), None),
            P(("groups", "blk"), None, None),
            P(("groups", "blk")),
        ),
        out_specs=P(("groups", "blk"), None),
        check_vma=False,
    )
```

time: 399 us -> 170 us (0.43)
  the two profiles are of different devices: /device:TPU:1 before, /device:TPU:3 now
where the time goes in v1:
time: 170 us; the launch traced here: 168 us
  waiting for transfers between devices  62.4 us (37%)
  Pallas kernels  53.5 us (31%)
  starting transfers between devices  35.5 us (21%)
  other arithmetic  7.96 us (5%)
  local copies, waits for them, and re-layouts  7.52 us (4%)
    pallas_call x4, Pallas kernels, meet(): pl.pallas_call(functools.partial(meet_kernel, n_gal, topk, float(width) *...  53.5 us
    ppermute x1, waiting for transfers between devices, on_device(): enc_near = lax.ppermute(enc_near.T, 'blk', shift(2)).T  28.9 us
    ppermute x1, waiting for transfers between devices, on_device(): enc_far = lax.ppermute(enc_far.T, 'blk', odd_shift(4)).T  20.1 us
    ppermute x1, starting transfers between devices, on_device(): live = jnp.concatenate([counts, lax.ppermute(counts, 'blk', swap)])  14.6 us
    ppermute x2, waiting for transfers between devices, on_device(): mass = lax.ppermute(mass[:, 0], 'blk', shift(-2))  13.1 us
    ppermute x1, starting transfers between devices, on_device(): mass_far = lax.ppermute(mass_far[:, 0], 'blk', odd_shift(-4))  3.71 us
    ppermute x1, starting transfers between devices, on_device(): total_far = lax.ppermute(total_far, 'blk', odd_shift(-4))  3.53 us
  transfers between devices with their start and end apart: 13, of which 4 were waited for; matrix products, arithmetic and copies ran while one was open for 5% of the time, Pallas kernels for 32%

profile of v1, /device:TPU:3, one launch (start us, length us, event | category | flops | bytes accessed | tf_op | source)
XLA Modules:
  0.0 167.8 jit_solution(3270867881289029233)
XLA Ops:
  0.0 0.7 collective-permute-start.3
  0.7 3.2 %collective-permute-start.1 = (bf16[512,2048]{1,0:T(8,128)(2,1)}, bf16[512,2048]{1,0:T(8,128)(2,1)}, u32[]{:S(2)}, u32[]{:S(2)}) collective-permute-start(bf16[512,2048]{1,0:T(8,128)(2,1)} %q_ref.1), channel_id=1, source_target_pairs={{0,0},{1,5},{2,2},{3,7},{4,4},{5,9},{6,6},{7,11},{8,8},{9,13},{10,... | collective-permute-start | bytes 6291464 | tf_op jit(solution)/shard_map/ppermute | solution.py:109
  3.9 2.8 %fusion.2 = (bf16[256,2048]{1,0:T(8,128)(2,1)S(1)}, bf16[256,2048]{1,0:T(8,128)(2,1)}) fusion(bf16[512,2048]{1,0:T(8,128)(2,1)} %q_ref.1), kind=kLoop, calls=%fused_computation.19 | loop fusion | bytes 4194304 | tf_op jit(solution)/shard_map/slice | solution.py:124
  6.7 1.3 collective-permute-start.10
  8.0 0.3 copy.18
  8.5 0.3 copy.17
  8.9 0.2 fusion.1
  9.1 0.4 copy.19
  9.7 0.8 slice_bitcast_fusion.1
  10.6 1.3 collective-permute-start.6
  11.9 14.6 %collective-permute-start = (s32[1]{0:T(128)}, s32[1]{0:T(128)}, u32[]{:S(2)}, u32[]{:S(2)}) collective-permute-start(s32[1]{0:T(128)} %param.7), channel_id=1, source_target_pairs={{0,1},{1,0},{2,3},{3,2},{4,5},{5,4},{6,7},{7,6},{8,9},{9,8},{10,11... | collective-permute-start | bytes 20 | tf_op jit(solution)/shard_map/ppermute | solution.py:111
  27.2 0.3 collective-permute-done.live_ref
  27.5 1.3 collective-permute-start.5
  28.8 1.2 pad_add_fusion.live_ref
  30.0 28.9 %collective-permute-done.6 = s32[16,512]{0,1:T(8,128)S(1)} collective-permute-done((s32[16,512]{0,1:T(8,128)S(1)}, s32[16,512]{0,1:T(8,128)S(1)}, u32[]{:S(2)}, u32[]{:S(2)}) %collective-permute-start.6) | collective-permute-done | bytes 32800 | tf_op jit(solution)/shard_map/ppermute | solution.py:107
  58.9 3.2 %collective-permute-start.2 = (s32[8,512]{0,1:T(8,128)S(1)}, s32[8,512]{0,1:T(8,128)S(1)}, u32[]{:S(2)}, u32[]{:S(2)}) collective-permute-start(s32[8,512]{0,1:T(8,128)S(1)} %get-tuple-element.29), channel_id=1, source_target_pairs={{0,0},{1,5},{2,2},{3,7},{4,4},{5,9},{6,6},{7,11},{8,8},{9,13},{10,... | collective-permute-start | bytes 49160 | tf_op jit(solution)/shard_map/ppermute | solution.py:108
  62.1 0.7 fusion.3
  62.8 20.1 %collective-permute-done.2 = s32[8,512]{0,1:T(8,128)S(1)} collective-permute-done((s32[8,512]{0,1:T(8,128)S(1)}, s32[8,512]{0,1:T(8,128)S(1)}, u32[]{:S(2)}, u32[]{:S(2)}) %collective-permute-start.2) | collective-permute-done | bytes 16416 | tf_op jit(solution)/shard_map/ppermute | solution.py:108
  82.9 0.7 copy-done.6
  83.6 13.2 %shard_map.47 = (bf16[512,2048]{1,0:T(8,128)(2,1)}, f32[512,1]{1,0:T(8,128)}) custom-call(s32[1]{0:T(128)} %collective-permute-done.live_ref, bf16[512,2048]{1,0:T(8,128)(2,1)} %collective-permute-done.1.q_ref, s32[512,8]{1,0:T(8,128)} %bitcast.15, bf16[1536,2048]{1,0:T(8,128)(2,1)} %collective-permute-done.3.refs_0_.refs_1_), custom_call_target="tpu_custom_call" | custom-call | flops 6442450944 | bytes 10485760 | tf_op jit(solution)/shard_map/pallas_call | solution.py:55
  96.8 3.5 %collective-permute-start.4 = (bf16[512,2048]{1,0:T(8,128)(2,1)}, bf16[512,2048]{1,0:T(8,128)(2,1)}, u32[]{:S(2)}, u32[]{:S(2)}) collective-permute-start(bf16[512,2048]{1,0:T(8,128)(2,1)} %get-tuple-element.14), channel_id=1, source_target_pairs={{0,0},{1,13},{2,2},{3,15},{4,4},{5,1},{6,6},{7,3},{8,8},{9,5},{10,... | collective-permute-start | bytes 6291464 | tf_op jit(solution)/shard_map/ppermute | solution.py:115
  100.4 13.8 %shard_map.49 = (bf16[256,2048]{1,0:T(8,128)(2,1)}, f32[256,1]{1,0:T(8,128)}) custom-call(s32[2]{0:T(128)} %pad_add_fusion.live_ref, bf16[256,2048]{1,0:T(8,128)(2,1)} %collective-permute-done.10.q_ref, s32[256,16]{1,0:T(8,128)} %get-tuple-element.32.enc_ref, bf16[1536,2048]{1,0:T(8,128)(2,1)} %refs_0_.5, ...), custom_call_target="tpu_custom_call" | custom-call | flops 6442450944 | bytes 14680064 | tf_op jit(solution)/shard_map/pallas_call | solution.py:55
  114.2 1.0 copy-done.5
  115.2 13.7 %shard_map.48 = (bf16[256,2048]{1,0:T(8,128)(2,1)}, f32[256,1]{1,0:T(8,128)}) custom-call(s32[2]{0:T(128)} %pad_add_fusion.live_ref, bf16[256,2048]{1,0:T(8,128)(2,1)} %copy-done.5, s32[256,16]{1,0:T(8,128)} %get-tuple-element.31.enc_ref, bf16[1536,2048]{1,0:T(8,128)(2,1)} %refs_0_.5, bf16[1536,2048]{1,0:T(8,128)(2,1)} %collective-permute-done.3.refs_0_.refs_1_), custom_call_target="tpu_custom_call" | custom-call | flops 6442450944 | bytes 14680064 | tf_op jit(solution)/shard_map/pallas_call | solution.py:55
  128.9 1.3 collective-permute-start.7
  130.5 12.8 %shard_map.46 = (bf16[512,2048]{1,0:T(8,128)(2,1)}, f32[512,1]{1,0:T(8,128)}) custom-call(s32[1]{0:T(128)S(6)} %copy.20.live_ref, bf16[512,2048]{1,0:T(8,128)(2,1)} %q_ref.1, s32[512,8]{1,0:T(8,128)} %get-tuple-element.27.enc_ref, bf16[1536,2048]{1,0:T(8,128)(2,1)} %refs_0_.5), custom_call_target="tpu_custom_call" | custom-call | flops 6442450944 | bytes 10485760 | tf_op jit(solution)/shard_map/pallas_call | solution.py:55
  143.4 1.3 collective-permute-start.8
  144.9 13.1 %collective-permute-done.12 = f32[256]{0:T(256)S(1)} collective-permute-done((f32[256]{0:T(256)S(1)}, f32[256]{0:T(256)S(1)}, u32[]{:S(2)}, u32[]{:S(2)}) %collective-permute-start.12) | collective-permute-done | bytes 1056 | tf_op jit(solution)/shard_map/ppermute | solution.py:122
  157.9 3.7 %collective-permute-start.9 = (f32[512]{0:T(512)S(1)}, f32[512]{0:T(512)S(1)}, u32[]{:S(2)}, u32[]{:S(2)}) collective-permute-start(f32[512]{0:T(512)S(1)} %reduce.2), channel_id=1, source_target_pairs={{0,0},{1,13},{2,2},{3,15},{4,4},{5,1},{6,6},{7,3},{8,8},{9,5},{10,... | collective-permute-start | bytes 6152 | tf_op jit(solution)/shard_map/ppermute | solution.py:116
  161.6 1.1 slice_reduce_fusion.1
  162.8 3.3 %divide_convert_fusion.1 = (bf16[256,2048]{1,0:T(8,128)(2,1)S(1)}, bf16[256,2048]{1,0:T(8,128)(2,1)S(1)}) fusion(bf16[256,2048]{1,0:T(8,128)(2,1)S(1)} %collective-permute-done.7, bf16[512,2048]{1,0:T(8,128)(2,1)} %collective-permute-done.4, f32[256]{0:T(256)S(1)} %get-tuple-element.33, bf16[512,2048]{1,0:T(8,128)(2,1)} %get-tuple-element.13, ...), kind=kLoop, calls=%fused_computation.2 | loop fusion | flops 9437184 | bytes 10487808 | tf_op jit(solution)/shard_map/convert_element_type | solution.py:125
  166.2 1.6 pad_maximum_fusion
  (31 shorter events, 1.0 us)
Async XLA Ops:
  0.0 8.0 %copy-start.1 = (s32[512,4,8]{0,2,1:T(8,128)S(1)}, s32[512,4,8]{0,2,1:T(8,128)}, u32[]{:S(2)}) copy-start(s32[512,4,8]{0,2,1:T(8,128)} %param.6) | copy-start | bytes 196612
  0.0 82.9 %collective-permute-start.3 = (bf16[1536,2048]{1,0:T(8,128)(2,1)}, bf16[1536,2048]{1,0:T(8,128)(2,1)}, u32[]{:S(2)}, u32[]{:S(2)}) collective-permute-start(bf16[1536,2048]{1,0:T(8,128)(2,1)} %refs_0_.5), channel_id=1, source_target_pairs={{0,1},{1,0},{2,3},{3,2},{4,5},{5,4},{6,7},{7,6},{8,9},{9,8},{10,11... | collective-permute-start | bytes 18874376 | tf_op jit(solution)/shard_map/ppermute | solution.py:110
  0.7 82.2 %collective-permute-start.1 = (bf16[512,2048]{1,0:T(8,128)(2,1)}, bf16[512,2048]{1,0:T(8,128)(2,1)}, u32[]{:S(2)}, u32[]{:S(2)}) collective-permute-start(bf16[512,2048]{1,0:T(8,128)(2,1)} %q_ref.1), channel_id=1, source_target_pairs={{0,0},{1,5},{2,2},{3,7},{4,4},{5,9},{6,6},{7,11},{8,8},{9,13},{10,... | collective-permute-start | bytes 6291464 | tf_op jit(solution)/shard_map/ppermute | solution.py:109
  6.7 93.7 %collective-permute-start.10 = (bf16[256,2048]{1,0:T(8,128)(2,1)}, bf16[256,2048]{1,0:T(8,128)(2,1)}, u32[]{:S(2)}, u32[]{:S(2)}) collective-permute-start(bf16[256,2048]{1,0:T(8,128)(2,1)} %get-tuple-element.26), channel_id=1, source_target_pairs={{0,2},{1,3},{2,4},{3,5},{4,6},{5,7},{6,8},{7,9},{8,10},{9,11},{10,... | collective-permute-start | bytes 3145736 | tf_op jit(solution)/shard_map/ppermute | solution.py:106
  10.6 48.2 %collective-permute-start.6 = (s32[16,512]{0,1:T(8,128)S(1)}, s32[16,512]{0,1:T(8,128)S(1)}, u32[]{:S(2)}, u32[]{:S(2)}) collective-permute-start(s32[16,512]{0,1:T(8,128)S(1)} %add_bitcast_fusion), channel_id=1, source_target_pairs={{0,2},{1,3},{2,4},{3,5},{4,6},{5,7},{6,8},{7,9},{8,10},{9,11},{10,... | collective-permute-start | bytes 98312 | tf_op jit(solution)/shard_map/ppermute | solution.py:107
  11.9 15.6 %collective-permute-start = (s32[1]{0:T(128)}, s32[1]{0:T(128)}, u32[]{:S(2)}, u32[]{:S(2)}) collective-permute-start(s32[1]{0:T(128)} %param.7), channel_id=1, source_target_pairs={{0,1},{1,0},{2,3},{3,2},{4,5},{5,4},{6,7},{7,6},{8,9},{9,8},{10,11... | collective-permute-start | bytes 20 | tf_op jit(solution)/shard_map/ppermute | solution.py:111
  27.5 86.7 %collective-permute-start.5 = (bf16[256,2048]{1,0:T(8,128)(2,1)S(1)}, bf16[256,2048]{1,0:T(8,128)(2,1)S(1)}, u32[]{:S(2)}, u32[]{:S(2)}) collective-permute-start(bf16[256,2048]{1,0:T(8,128)(2,1)S(1)} %get-tuple-element.25), channel_id=1, source_target_pairs={{0,2},{1,3},{2,4},{3,5},{4,6},{5,7},{6,8},{7,9},{8,10},{9,11},{10,... | collective-permute-start | bytes 3145736 | tf_op jit(solution)/shard_map/ppermute | solution.py:106
  58.9 24.0 %collective-permute-start.2 = (s32[8,512]{0,1:T(8,128)S(1)}, s32[8,512]{0,1:T(8,128)S(1)}, u32[]{:S(2)}, u32[]{:S(2)}) collective-permute-start(s32[8,512]{0,1:T(8,128)S(1)} %get-tuple-element.29), channel_id=1, source_target_pairs={{0,0},{1,5},{2,2},{3,7},{4,4},{5,9},{6,6},{7,11},{8,8},{9,13},{10,... | collective-permute-start | bytes 49160 | tf_op jit(solution)/shard_map/ppermute | solution.py:108
  82.9 0.7 copy-start.6
  96.8 66.0 %collective-permute-start.4 = (bf16[512,2048]{1,0:T(8,128)(2,1)}, bf16[512,2048]{1,0:T(8,128)(2,1)}, u32[]{:S(2)}, u32[]{:S(2)}) collective-permute-start(bf16[512,2048]{1,0:T(8,128)(2,1)} %get-tuple-element.14), channel_id=1, source_target_pairs={{0,0},{1,13},{2,2},{3,15},{4,4},{5,1},{6,6},{7,3},{8,8},{9,5},{10,... | collective-permute-start | bytes 6291464 | tf_op jit(solution)/shard_map/ppermute | solution.py:115
  114.2 48.6 %collective-permute-start.11 = (bf16[256,2048]{1,0:T(8,128)(2,1)}, bf16[256,2048]{1,0:T(8,128)(2,1)}, u32[]{:S(2)}, u32[]{:S(2)}) collective-permute-start(bf16[256,2048]{1,0:T(8,128)(2,1)} %get-tuple-element.19), channel_id=1, source_target_pairs={{0,14},{1,15},{2,0},{3,1},{4,2},{5,3},{6,4},{7,5},{8,6},{9,7},{10,... | collective-permute-start | bytes 3145736 | tf_op jit(solution)/shard_map/ppermute | solution.py:121
  114.2 1.0 copy-start.5
  115.2 15.1 %copy-start.3 = (f32[256,1]{1,0:T(8,128)S(1)}, f32[256,1]{1,0:T(8,128)}, u32[]{:S(2)}) copy-start(f32[256,1]{1,0:T(8,128)} %get-tuple-element.20) | copy-start | bytes 3076
  128.9 33.9 %collective-permute-start.7 = (bf16[256,2048]{1,0:T(8,128)(2,1)}, bf16[256,2048]{1,0:T(8,128)(2,1)S(1)}, u32[]{:S(2)}, u32[]{:S(2)}) collective-permute-start(bf16[256,2048]{1,0:T(8,128)(2,1)} %get-tuple-element.15), channel_id=1, source_target_pairs={{0,14},{1,15},{2,0},{3,1},{4,2},{5,3},{6,4},{7,5},{8,6},{9,7},{10,... | collective-permute-start | bytes 3145736 | tf_op jit(solution)/shard_map/ppermute | solution.py:121
  130.4 27.6 %collective-permute-start.12 = (f32[256]{0:T(256)S(1)}, f32[256]{0:T(256)S(1)}, u32[]{:S(2)}, u32[]{:S(2)}) collective-permute-start(f32[256]{0:T(256)S(1)} %reduce.3), channel_id=1, source_target_pairs={{0,14},{1,15},{2,0},{3,1},{4,2},{5,3},{6,4},{7,5},{8,6},{9,7},{10,... | collective-permute-start | bytes 3080 | tf_op jit(solution)/shard_map/ppermute | solution.py:122
  130.4 12.8 %copy-start.4 = (f32[256,1]{1,0:T(8,128)S(1)}, f32[256,1]{1,0:T(8,128)}, u32[]{:S(2)}) copy-start(f32[256,1]{1,0:T(8,128)} %get-tuple-element.16) | copy-start | bytes 3076
  130.4 14.3 %copy-start.2 = (f32[512,1]{1,0:T(8,128)S(1)}, f32[512,1]{1,0:T(8,128)}, u32[]{:S(2)}) copy-start(f32[512,1]{1,0:T(8,128)} %get-tuple-element.18) | copy-start | bytes 6148
  130.5 32.4 %copy-start = (bf16[512,2048]{1,0:T(8,128)(2,1)S(1)}, bf16[512,2048]{1,0:T(8,128)(2,1)}, u32[]{:S(2)}) copy-start(bf16[512,2048]{1,0:T(8,128)(2,1)} %q_ref.1) | copy-start | bytes 6291460
  143.4 19.4 %collective-permute-start.8 = (f32[256]{0:T(256)S(1)}, f32[256]{0:T(256)S(1)}, u32[]{:S(2)}, u32[]{:S(2)}) collective-permute-start(f32[256]{0:T(256)S(1)} %reduce), channel_id=1, source_target_pairs={{0,14},{1,15},{2,0},{3,1},{4,2},{5,3},{6,4},{7,5},{8,6},{9,7},{10,... | collective-permute-start | bytes 3080 | tf_op jit(solution)/shard_map/ppermute | solution.py:122
  157.9 4.8 %collective-permute-start.9 = (f32[512]{0:T(512)S(1)}, f32[512]{0:T(512)S(1)}, u32[]{:S(2)}, u32[]{:S(2)}) collective-permute-start(f32[512]{0:T(512)S(1)} %reduce.2), channel_id=1, source_target_pairs={{0,0},{1,13},{2,2},{3,15},{4,4},{5,1},{6,6},{7,3},{8,8},{9,5},{10,... | collective-permute-start | bytes 6152 | tf_op jit(solution)/shard_map/ppermute | solution.py:116

commit v2 on v1

v2 whole, which is shorter than its diff:
```python
import functools

import jax
import jax.numpy as jnp
from jax import lax
from jax.experimental import pallas as pl
from jax.experimental.pallas import tpu as pltpu
from jax.sharding import PartitionSpec as P

CHUNKS = 2
ORDER = (("near", 0), ("far", 0), ("far", 1), ("near", 1))
TILE = 256
TAIL = 16
BASE = 256
VMEM_BYTES = 65000 * 1024


def cost(flops):
    return pl.CostEstimate(flops=flops, bytes_accessed=flops // 64, transcendentals=0)


def pack_kernel(q_ref, picks_ref, out_ref):
    steps, topk, rows = picks_ref.shape
    out_ref[:rows, :] = q_ref[...]
    out_ref[rows:, :] = jnp.zeros((TAIL, out_ref.shape[1]), out_ref.dtype)
    for s in range(steps):
        picks = picks_ref[s]
        halves = [(picks >> 8).astype(jnp.float32), (picks & (BASE - 1)).astype(jnp.float32)]
        out_ref[rows:, s * rows : (s + 1) * rows] = jnp.concatenate(halves, axis=0).astype(out_ref.dtype)


def pack(queries, picks, first, rows):
    width = queries.shape[1]
    at = first // rows
    return pl.pallas_call(
        pack_kernel,
        grid=(1,),
        out_shape=jax.ShapeDtypeStruct((rows + TAIL, width), queries.dtype),
        in_specs=[
            pl.BlockSpec((rows, width), lambda i: (at, 0)),
            pl.BlockSpec((*picks.shape[:2], rows), lambda i: (0, 0, at)),
        ],
        out_specs=pl.BlockSpec((rows + TAIL, width), lambda i: (0, 0)),
        compiler_params=pltpu.CompilerParams(vmem_limit_bytes=VMEM_BYTES),
        cost_estimate=cost(rows * width),
    )(queries, picks)


def unpack(tail, topk):
    parts = tail.astype(jnp.float32)
    return (parts[:topk] * BASE + parts[topk:]).astype(jnp.int32)


def pick_table(picks, live, scale3):
    topk = picks.shape[0]
    place = lax.broadcasted_iota(jnp.int32, picks.shape, 0)
    many = jnp.ones(picks.shape, jnp.float32)
    keep = picks < live
    for turn in range(1, topk):
        same = picks == pltpu.roll(picks, turn, 0)
        many = many + jnp.where(same, 1.0, 0.0)
        keep = keep & jnp.logical_not(same & (place >= turn))
    return jnp.where(keep, picks, -1).T, (many * scale3).T


def meet_kernel(n_src, gal_ids, scale3, topk, core_ref, live_ref, token_ref, *refs):
    n_gal = len(gal_ids)
    even = core_ref[0] == 0
    sources = [refs[i * (1 + 2 * n_gal) : (i + 1) * (1 + 2 * n_gal)] for i in range(n_src)]
    refs = refs[n_src * (1 + 2 * n_gal) :]
    gal_refs, refs = refs[:n_gal], refs[n_gal:]
    out_ref, w_ref = refs[:2]
    q_ref = sources[0][0]
    rows = q_ref.shape[0]
    if n_src == 2:
        far_ref, q_ref = sources[1][0], refs[2]

        @pl.when(even)
        def _():
            q_ref[...] = sources[0][0][...]

        @pl.when(jnp.logical_not(even))
        def _():
            q_ref[...] = far_ref[...]

    gal_rows, width = gal_refs[0].shape
    mass = jnp.zeros((rows, 128), jnp.float32)
    for g in range(n_gal):
        first, last = sources[0][1 + 2 * g], sources[-1][2 + 2 * g]
        if len(first.shape) == 3:
            picks = first[0]
        else:
            picks = jnp.where(even, unpack(first[...], topk), unpack(last[...], topk))
        pick, gain = pick_table(picks, live_ref[gal_ids[g]], scale3)
        for t in range(gal_rows // TILE):
            tile = gal_refs[g][t * TILE : (t + 1) * TILE, :]
            s = lax.dot_general(q_ref[...], tile, (((1,), (1,)), ((), ())), preferred_element_type=jnp.float32)
            col = lax.broadcasted_iota(jnp.int32, (rows, TILE), 1) + t * TILE
            c = jnp.zeros((rows, TILE), jnp.float32)
            for k in range(topk):
                c = jnp.where(col == pick[:, k : k + 1], gain[:, k : k + 1], c)
            r = jnp.maximum(s, 0.0)
            w = r * r * (r * c)
            for j in range(TILE // 128):
                mass = mass + w[:, j * 128 : (j + 1) * 128]
            w_ref[g, :, t * TILE : (t + 1) * TILE] = w.astype(jnp.bfloat16)
    for n in range(width // TILE):
        cut = slice(n * TILE, (n + 1) * TILE)
        total = jnp.dot(w_ref[0], gal_refs[0][:, cut], preferred_element_type=jnp.float32)
        for g in range(1, n_gal):
            total = total + jnp.dot(w_ref[g], gal_refs[g][:, cut], preferred_element_type=jnp.float32)
        out_ref[:rows, cut] = total.astype(out_ref.dtype)
    mass = jnp.sum(mass.T, axis=0, keepdims=True)
    high = mass.astype(jnp.bfloat16).astype(jnp.float32)
    mid = (mass - high).astype(jnp.bfloat16).astype(jnp.float32)
    part = lax.broadcasted_iota(jnp.int32, (TAIL, rows), 0)
    tail = jnp.where(part == 0, high, jnp.where(part == 1, mid, jnp.where(part == 2, mass - high - mid, 0.0)))
    out_ref[rows:, :] = jnp.zeros((TAIL, width), out_ref.dtype)
    out_ref[rows:, :rows] = tail.astype(out_ref.dtype)


def meet(core, lives, token, sources, gals, steps, rows, at, topk):
    gal_rows, width = gals[0].shape
    n_gal = len(gals)
    operands, specs = [], []
    for source in sources:
        raw = isinstance(source, tuple)
        queries = source[0] if raw else source
        operands.append(queries)
        specs.append(pl.BlockSpec((rows, width), functools.partial(lambda o, i: (o, 0), at if raw else 0)))
        for _, *both in steps:
            for step in both:
                if raw:
                    operands.append(source[1])
                    specs.append(pl.BlockSpec((1, topk, rows), functools.partial(lambda s, i: (s, 0, at), step)))
                else:
                    operands.append(queries)
                    specs.append(
                        pl.BlockSpec((TAIL, rows), functools.partial(lambda s, i: (rows // TAIL, s), step))
                    )
    scratch = [pltpu.VMEM((n_gal, rows, gal_rows), jnp.bfloat16)]
    if len(sources) == 2:
        scratch.append(pltpu.VMEM((rows, width), jnp.bfloat16))
    return pl.pallas_call(
        functools.partial(meet_kernel, len(sources), tuple(s[0] for s in steps), float(width) ** -1.5, topk),
        grid=(1,),
        out_shape=jax.ShapeDtypeStruct((rows + TAIL, width), jnp.bfloat16),
        in_specs=[
            pl.BlockSpec(memory_space=pltpu.SMEM),
            pl.BlockSpec(memory_space=pltpu.SMEM),
            pl.BlockSpec(memory_space=pl.ANY),
        ]
        + specs
        + [pl.BlockSpec((gal_rows, width), lambda i: (0, 0))] * n_gal,
        out_specs=pl.BlockSpec((rows + TAIL, width), lambda i: (0, 0)),
        scratch_shapes=scratch,
        compiler_params=pltpu.CompilerParams(vmem_limit_bytes=VMEM_BYTES),
        cost_estimate=cost(rows * width),
    )(core, lives, token, *operands, *gals)


def finish_kernel(core_ref, q_ref, own_ref, own_tail, near_ref, near_tail, far_ref, far_tail, back_ref, back_tail, *refs):
    out_ref = refs[-1]
    rows = q_ref.shape[0]
    even = core_ref[0] == 0

    def write(far_ref, far_tail):
        tails = own_tail[...].astype(jnp.float32) + near_tail[...].astype(jnp.float32) + far_tail[...].astype(jnp.float32)
        mass = 1.0 + jnp.sum(tails.T, axis=1, keepdims=True)
        total = own_ref[...].astype(jnp.float32) + near_ref[...].astype(jnp.float32) + far_ref[...].astype(jnp.float32)
        out_ref[...] = ((q_ref[...].astype(jnp.float32) + total) / mass).astype(out_ref.dtype)

    @pl.when(even)
    def _():
        write(far_ref, far_tail)

    @pl.when(jnp.logical_not(even))
    def _():
        write(back_ref, back_tail)


def finish(core, at, rows, queries, own, near, far, back, done, block=128):
    width = queries.shape[1]
    per = rows // block
    first = at * per
    operands, specs = [queries], [pl.BlockSpec((block, width), lambda i: (first + i, 0))]
    for array, begin in ((own, first), (near, 0), (far, 0), (back, 0)):
        tail_row = (array.shape[0] - TAIL) // TAIL
        operands += [array, array]
        specs.append(pl.BlockSpec((block, width), functools.partial(lambda o, i: (o + i, 0), begin)))
        specs.append(pl.BlockSpec((TAIL, block), functools.partial(lambda t, o, i: (t, o + i), tail_row, begin)))
    extra = {}
    if done is not None:
        operands.append(done)
        specs.append(pl.BlockSpec(memory_space=pl.ANY))
        extra = {"input_output_aliases": {len(operands): 0}}
    return pl.pallas_call(
        finish_kernel,
        grid=(per,),
        out_shape=jax.ShapeDtypeStruct(queries.shape, queries.dtype),
        in_specs=[pl.BlockSpec(memory_space=pltpu.SMEM)] + specs,
        out_specs=pl.BlockSpec((block, width), lambda i: (first + i, 0)),
        compiler_params=pltpu.CompilerParams(vmem_limit_bytes=VMEM_BYTES),
        cost_estimate=cost(rows * width),
        **extra,
    )(core, *operands)


def on_device(queries, gallery, neighbors, counts):
    n = lax.axis_size("blk")
    core = jnp.reshape(lax.axis_index("blk") % 2, (1,)).astype(jnp.int32)
    rows, width = queries.shape
    topk = neighbors.shape[2]
    picks = jnp.transpose(neighbors, (1, 2, 0))

    def shift(k):
        return [(i, (i + k) % n) for i in range(n)]

    def odd_shift(k):
        return [(i, (i + k) % n) for i in range(1, n, 2)]

    swap = [(i, i ^ 1) for i in range(n)]

    size = rows // CHUNKS
    packed = [pack(queries, picks, c * size, size) for c in range(CHUNKS)]
    near = [lax.ppermute(chunk, "blk", shift(2)) for chunk in packed]
    other = lax.ppermute(gallery, "blk", swap)
    live = jnp.concatenate([counts, lax.ppermute(counts, "blk", swap)])
    far = [lax.ppermute(chunk, "blk", odd_shift(4)) for chunk in packed]

    own = meet(core, counts, packed[-1], [(queries, picks)], (gallery,), ((0, 0, 0),), rows, 0, topk)
    token = own
    near_back, far_here, far_back = {}, {}, {}
    for kind, c in ORDER:
        if kind == "near":
            token = meet(core, live, token, [near[c]], (gallery, other), ((0, 2, 2), (1, 3, 1)), size, 0, topk)
            near_back[c] = lax.ppermute(token, "blk", shift(-2))
        else:
            token = meet(core, live, token, [packed[c], far[c]], (other,), ((1, 1, 3),), size, 0, topk)
            far_here[c] = token
            far_back[c] = lax.ppermute(token, "blk", odd_shift(-4))
    done = None
    for c in range(CHUNKS):
        done = finish(core, c, size, queries, own, near_back[c], far_here[c], far_back[c], done)
    return done


def solution(mesh):
    return jax.shard_map(
        on_device,
        mesh=mesh,
        in_specs=(
            P(("groups", "blk"), None),
            P(("groups", "blk"), None),
            P(("groups", "blk"), None, None),
            P(("groups", "blk")),
        ),
        out_specs=P(("groups", "blk"), None),
        check_vma=False,
    )
```

time: 170 us -> 137 us (0.81)
  the two profiles are of different devices: /device:TPU:3 before, /device:TPU:1 now
where the time goes in v2:
time: 137 us
  Pallas kernels  70.8 us (52%)
  waiting for transfers between devices  35.2 us (26%)
  starting transfers between devices  28.9 us (21%)
    pallas_call x5, Pallas kernels, meet(): pl.pallas_call(functools.partial(meet_kernel, len(sources), tuple((s[0] f...  58.8 us
    ppermute x2, starting transfers between devices, on_device(): far_back[c] = lax.ppermute(token, 'blk', odd_shift(-4))  16 us
    ppermute x2, waiting for transfers between devices, on_device(): near = [lax.ppermute(chunk, 'blk', shift(2)) for chunk in packed]  14.9 us
    ppermute x2, waiting for transfers between devices, on_device(): far_back[c] = lax.ppermute(token, 'blk', odd_shift(-4))  13.2 us
    pallas_call x2, Pallas kernels, finish(): pl.pallas_call(finish_kernel, grid=(per,), out_shape=jax.ShapeDtypeStruct...  7.39 us
    ppermute x2, starting transfers between devices, on_device(): far = [lax.ppermute(chunk, 'blk', odd_shift(4)) for chunk in packed]  6.39 us
    ppermute x2, waiting for transfers between devices, on_device(): near_back[c] = lax.ppermute(token, 'blk', shift(-2))  5.72 us
    pallas_call x2, Pallas kernels, pack(): pl.pallas_call(pack_kernel, grid=(1,), out_shape=jax.ShapeDtypeStruct((ro...  4.62 us
  transfers between devices with their start and end apart: 10, of which 5 were waited for; matrix products, arithmetic and copies ran while one was open for 1% of the time, Pallas kernels for 49%

profile of v2, /device:TPU:1, one launch (start us, length us, event | category | flops | bytes accessed | tf_op | source)
XLA Modules:
  0.0 136.8 jit_solution(8019948465958582909)
XLA Ops:
  0.0 0.1 collective-permute-start.2
  0.1 2.3 %shard_map.48.refs_0_.refs_1_.refs_2_ = bf16[272,2048]{1,0:T(8,128)(2,1)} custom-call(bf16[512,2048]{1,0:T(8,128)(2,1)} %q_ref.7, s32[4,8,512]{2,1,0:T(8,128)} %bitcast.2), custom_call_target="tpu_custom_call" | custom-call | flops 524288 | bytes 8192 | tf_op jit(solution)/shard_map/pallas_call | solution.py:35
  2.4 2.7 %collective-permute-start.1 = (bf16[272,2048]{1,0:T(8,128)(2,1)}, bf16[272,2048]{1,0:T(8,128)(2,1)}, u32[]{:S(2)}, u32[]{:S(2)}) collective-permute-start(bf16[272,2048]{1,0:T(8,128)(2,1)} %shard_map.48.refs_0_.refs_1_.refs_2_), channel_id=1, source_target_pairs={{0,2},{1,3},{2,4},{3,5},{4,6},{5,7},{6,8},{7,9},{8,10},{9,11},{10,... | collective-permute-start | bytes 3342344 | tf_op jit(solution)/shard_map/ppermute | solution.py:226
  5.0 3.2 %collective-permute-start.3 = (bf16[272,2048]{1,0:T(8,128)(2,1)}, bf16[272,2048]{1,0:T(8,128)(2,1)}, u32[]{:S(2)}, u32[]{:S(2)}) collective-permute-start(bf16[272,2048]{1,0:T(8,128)(2,1)} %shard_map.48.refs_0_.refs_1_.refs_2_), channel_id=1, source_target_pairs={{1,5},{3,7},{5,9},{7,11},{9,13},{11,15},{13,1},{15,3},{17,21},{19,... | collective-permute-start | bytes 3342344 | tf_op jit(solution)/shard_map/ppermute | solution.py:229
  8.2 2.3 %shard_map.46.token_ref.refs_0_.refs_1_.refs_2_ = bf16[272,2048]{1,0:T(8,128)(2,1)} custom-call(bf16[512,2048]{1,0:T(8,128)(2,1)} %q_ref.7, s32[4,8,512]{2,1,0:T(8,128)} %bitcast.3), custom_call_target="tpu_custom_call" | custom-call | flops 524288 | bytes 8192 | tf_op jit(solution)/shard_map/pallas_call | solution.py:35
  10.5 3.2 %collective-permute-start.4 = (bf16[272,2048]{1,0:T(8,128)(2,1)}, bf16[272,2048]{1,0:T(8,128)(2,1)}, u32[]{:S(2)}, u32[]{:S(2)}) collective-permute-start(bf16[272,2048]{1,0:T(8,128)(2,1)} %shard_map.46.token_ref.refs_0_.refs_1_.refs_2_), channel_id=1, source_target_pairs={{1,5},{3,7},{5,9},{7,11},{9,13},{11,15},{13,1},{15,3},{17,21},{19,... | collective-permute-start | bytes 3342344 | tf_op jit(solution)/shard_map/ppermute | solution.py:229
  13.7 0.1 collective-permute-start
  13.8 1.4 %collective-permute-done = s32[1]{0:T(128)} collective-permute-done((s32[1]{0:T(128)}, s32[1]{0:T(128)}, u32[]{:S(2)}, u32[]{:S(2)}) %collective-permute-start) | collective-permute-done | bytes 36 | tf_op jit(solution)/shard_map/ppermute | solution.py:228
  15.2 1.3 collective-permute-start.5
  17.1 13.0 %shard_map.47.token_ref.own_ref.own_tail = bf16[528,2048]{1,0:T(8,128)(2,1)} custom-call(s32[1]{0:T(128)} %bitcast.core_ref, s32[1]{0:T(128)S(6)} %copy.7.live_ref, bf16[272,2048]{1,0:T(8,128)(2,1)} %shard_map.46.token_ref.refs_0_.refs_1_.refs_2_, bf16[512,2048]{1,0:T(8,128)(2,1)} %q_ref.7, s32[4,8,512]{2,1,0:T(8,128)} %bitcast.4, s32[4,8,512]{2,1,0:T(8,128)} %bitcast.5, ...), custom_call_target="tpu_custom_call" | custom-call | flops 1048576 | bytes 16384 | tf_op jit(solution)/shard_map/pallas_call | solution.py:144
  30.1 1.2 pad_add_fusion.live_ref
  31.2 2.1 %collective-permute-done.1.refs_0_.refs_1_.refs_2_.refs_3_.refs_4_ = bf16[272,2048]{1,0:T(8,128)(2,1)} collective-permute-done((bf16[272,2048]{1,0:T(8,128)(2,1)}, bf16[272,2048]{1,0:T(8,128)(2,1)}, u32[]{:S(2)}, u32[]{:S(2)}) %collective-permute-start.1) | collective-permute-done | bytes 1114144 | tf_op jit(solution)/shard_map/ppermute | solution.py:226
  33.3 0.0 collective-permute-done.2.refs_6_
  33.3 14.4 %shard_map.49.token_ref = bf16[272,2048]{1,0:T(8,128)(2,1)} custom-call(s32[1]{0:T(128)} %bitcast.core_ref, s32[2]{0:T(128)} %pad_add_fusion.live_ref, bf16[528,2048]{1,0:T(8,128)(2,1)} %shard_map.47.token_ref.own_ref.own_tail, bf16[272,2048]{1,0:T(8,128)(2,1)} %collective-permute-done.1.refs_0_.refs_1_.refs_2_.refs_3_.refs_4_, ...), custom_call_target="tpu_custom_call" | custom-call | flops 524288 | bytes 8192 | tf_op jit(solution)/shard_map/pallas_call | solution.py:144
  47.7 1.3 collective-permute-start.8
  49.0 0.0 collective-permute-done.3.refs_3_.refs_4_.refs_5_
  49.0 8.7 %shard_map.50.token_ref.far_ref.far_tail = bf16[272,2048]{1,0:T(8,128)(2,1)} custom-call(s32[1]{0:T(128)} %bitcast.core_ref, s32[2]{0:T(128)} %pad_add_fusion.live_ref, bf16[272,2048]{1,0:T(8,128)(2,1)} %shard_map.49.token_ref, bf16[272,2048]{1,0:T(8,128)(2,1)} %shard_map.48.refs_0_.refs_1_.refs_2_, bf16[272,2048]{1,0:T(8,128)(2,1)} %shard_map.48.refs_0_.refs_1_.refs_2_, ...), custom_call_target="tpu_custom_call" | custom-call | flops 524288 | bytes 8192 | tf_op jit(solution)/shard_map/pallas_call | solution.py:144
  57.6 2.1 %collective-permute-start.9 = (bf16[272,2048]{1,0:T(8,128)(2,1)}, bf16[272,2048]{1,0:T(8,128)(2,1)}, u32[]{:S(2)}, u32[]{:S(2)}) collective-permute-start(bf16[272,2048]{1,0:T(8,128)(2,1)} %shard_map.50.token_ref.far_ref.far_tail), channel_id=1, source_target_pairs={{1,13},{3,15},{5,1},{7,3},{9,5},{11,7},{13,9},{15,11},{17,29},{19,... | collective-permute-start | bytes 3342344 | tf_op jit(solution)/shard_map/ppermute | solution.py:241
  59.7 0.0 collective-permute-done.4.refs_3_.refs_4_.refs_5_
  59.7 8.7 %shard_map.51.token_ref.far_ref.far_tail = bf16[272,2048]{1,0:T(8,128)(2,1)} custom-call(s32[1]{0:T(128)} %bitcast.core_ref, s32[2]{0:T(128)} %pad_add_fusion.live_ref, bf16[272,2048]{1,0:T(8,128)(2,1)} %shard_map.50.token_ref.far_ref.far_tail, bf16[272,2048]{1,0:T(8,128)(2,1)} %shard_map.46.token_ref.refs_0_.refs_1_.refs_2_, ...), custom_call_target="tpu_custom_call" | custom-call | flops 524288 | bytes 8192 | tf_op jit(solution)/shard_map/pallas_call | solution.py:144
  68.4 12.8 %collective-permute-done.5.refs_0_.refs_1_.refs_2_.refs_3_.refs_4_ = bf16[272,2048]{1,0:T(8,128)(2,1)} collective-permute-done((bf16[272,2048]{1,0:T(8,128)(2,1)}, bf16[272,2048]{1,0:T(8,128)(2,1)}, u32[]{:S(2)}, u32[]{:S(2)}) %collective-permute-start.5) | collective-permute-done | bytes 1114144 | tf_op jit(solution)/shard_map/ppermute | solution.py:226
  81.2 14.2 %shard_map.52 = bf16[272,2048]{1,0:T(8,128)(2,1)} custom-call(s32[1]{0:T(128)} %bitcast.core_ref, s32[2]{0:T(128)} %pad_add_fusion.live_ref, bf16[272,2048]{1,0:T(8,128)(2,1)} %shard_map.51.token_ref.far_ref.far_tail, bf16[272,2048]{1,0:T(8,128)(2,1)} %collective-permute-done.5.refs_0_.refs_1_.refs_2_.refs_3_.refs_4_, ...), custom_call_target="tpu_custom_call" | custom-call | flops 524288 | bytes 8192 | tf_op jit(solution)/shard_map/pallas_call | solution.py:144
  95.4 1.1 collective-permute-start.6
  96.5 14.0 %collective-permute-start.7 = (bf16[272,2048]{1,0:T(8,128)(2,1)}, bf16[272,2048]{1,0:T(8,128)(2,1)}, u32[]{:S(2)}, u32[]{:S(2)}) collective-permute-start(bf16[272,2048]{1,0:T(8,128)(2,1)} %shard_map.51.token_ref.far_ref.far_tail), channel_id=1, source_target_pairs={{1,13},{3,15},{5,1},{7,3},{9,5},{11,7},{13,9},{15,11},{17,29},{19,... | collective-permute-start | bytes 3342344 | tf_op jit(solution)/shard_map/ppermute | solution.py:241
  110.4 0.0 collective-permute-done.8.near_ref.near_tail
  110.5 0.0 collective-permute-done.9.back_ref.back_tail
  110.5 3.7 %shard_map.53.refs_0_ = bf16[512,2048]{1,0:T(8,128)(2,1)} custom-call(s32[1]{0:T(128)} %bitcast.core_ref, bf16[512,2048]{1,0:T(8,128)(2,1)} %q_ref.7, bf16[528,2048]{1,0:T(8,128)(2,1)} %shard_map.47.token_ref.own_ref.own_tail, bf16[528,2048]{1,0:T(8,128)(2,1)} %shard_map.47.token_ref.own_ref.own_tail, ...), custom_call_target="tpu_custom_call" | custom-call | flops 524288 | bytes 8192 | tf_op jit(solution)/shard_map/pallas_call | solution.py:197
  114.2 5.7 %collective-permute-done.6.near_ref.near_tail = bf16[272,2048]{1,0:T(8,128)(2,1)} collective-permute-done((bf16[272,2048]{1,0:T(8,128)(2,1)}, bf16[272,2048]{1,0:T(8,128)(2,1)}, u32[]{:S(2)}, u32[]{:S(2)}) %collective-permute-start.6) | collective-permute-done | bytes 1114144 | tf_op jit(solution)/shard_map/ppermute | solution.py:237
  119.9 13.2 %collective-permute-done.7.back_ref.back_tail = bf16[272,2048]{1,0:T(8,128)(2,1)} collective-permute-done((bf16[272,2048]{1,0:T(8,128)(2,1)}, bf16[272,2048]{1,0:T(8,128)(2,1)}, u32[]{:S(2)}, u32[]{:S(2)}) %collective-permute-start.7) | collective-permute-done | bytes 1114144 | tf_op jit(solution)/shard_map/ppermute | solution.py:241
  133.1 3.7 %shard_map.54 = bf16[512,2048]{1,0:T(8,128)(2,1)} custom-call(s32[1]{0:T(128)} %bitcast.core_ref, bf16[512,2048]{1,0:T(8,128)(2,1)} %q_ref.7, bf16[528,2048]{1,0:T(8,128)(2,1)} %shard_map.47.token_ref.own_ref.own_tail, bf16[528,2048]{1,0:T(8,128)(2,1)} %shard_map.47.token_ref.own_ref.own_tail, ...), custom_call_target="tpu_custom_call", output_to_operand_aliasing={{}: (10, {})} | custom-call | flops 524288 | bytes 8192 | tf_op jit(solution)/shard_map/pallas_call | solution.py:197
Async XLA Ops:
  0.0 33.3 %collective-permute-start.2 = (bf16[1536,2048]{1,0:T(8,128)(2,1)}, bf16[1536,2048]{1,0:T(8,128)(2,1)}, u32[]{:S(2)}, u32[]{:S(2)}) collective-permute-start(bf16[1536,2048]{1,0:T(8,128)(2,1)} %refs_5_.3), channel_id=1, source_target_pairs={{0,1},{1,0},{2,3},{3,2},{4,5},{5,4},{6,7},{7,6},{8,9},{9,8},{10,11... | collective-permute-start | bytes 18874376 | tf_op jit(solution)/shard_map/ppermute | solution.py:227
  2.4 30.9 %collective-permute-start.1 = (bf16[272,2048]{1,0:T(8,128)(2,1)}, bf16[272,2048]{1,0:T(8,128)(2,1)}, u32[]{:S(2)}, u32[]{:S(2)}) collective-permute-start(bf16[272,2048]{1,0:T(8,128)(2,1)} %shard_map.48.refs_0_.refs_1_.refs_2_), channel_id=1, source_target_pairs={{0,2},{1,3},{2,4},{3,5},{4,6},{5,7},{6,8},{7,9},{8,10},{9,11},{10,... | collective-permute-start | bytes 3342344 | tf_op jit(solution)/shard_map/ppermute | solution.py:226
  5.0 43.9 %collective-permute-start.3 = (bf16[272,2048]{1,0:T(8,128)(2,1)}, bf16[272,2048]{1,0:T(8,128)(2,1)}, u32[]{:S(2)}, u32[]{:S(2)}) collective-permute-start(bf16[272,2048]{1,0:T(8,128)(2,1)} %shard_map.48.refs_0_.refs_1_.refs_2_), channel_id=1, source_target_pairs={{1,5},{3,7},{5,9},{7,11},{9,13},{11,15},{13,1},{15,3},{17,21},{19,... | collective-permute-start | bytes 3342344 | tf_op jit(solution)/shard_map/ppermute | solution.py:229
  10.5 49.2 %collective-permute-start.4 = (bf16[272,2048]{1,0:T(8,128)(2,1)}, bf16[272,2048]{1,0:T(8,128)(2,1)}, u32[]{:S(2)}, u32[]{:S(2)}) collective-permute-start(bf16[272,2048]{1,0:T(8,128)(2,1)} %shard_map.46.token_ref.refs_0_.refs_1_.refs_2_), channel_id=1, source_target_pairs={{1,5},{3,7},{5,9},{7,11},{9,13},{11,15},{13,1},{15,3},{17,21},{19,... | collective-permute-start | bytes 3342344 | tf_op jit(solution)/shard_map/ppermute | solution.py:229
  13.7 1.5 %collective-permute-start = (s32[1]{0:T(128)}, s32[1]{0:T(128)}, u32[]{:S(2)}, u32[]{:S(2)}) collective-permute-start(s32[1]{0:T(128)} %param.7), channel_id=1, source_target_pairs={{0,1},{1,0},{2,3},{3,2},{4,5},{5,4},{6,7},{7,6},{8,9},{9,8},{10,11... | collective-permute-start | bytes 20 | tf_op jit(solution)/shard_map/ppermute | solution.py:228
  15.2 66.0 %collective-permute-start.5 = (bf16[272,2048]{1,0:T(8,128)(2,1)}, bf16[272,2048]{1,0:T(8,128)(2,1)}, u32[]{:S(2)}, u32[]{:S(2)}) collective-permute-start(bf16[272,2048]{1,0:T(8,128)(2,1)} %shard_map.46.token_ref.refs_0_.refs_1_.refs_2_), channel_id=1, source_target_pairs={{0,2},{1,3},{2,4},{3,5},{4,6},{5,7},{6,8},{7,9},{8,10},{9,11},{10,... | collective-permute-start | bytes 3342344 | tf_op jit(solution)/shard_map/ppermute | solution.py:226
  47.7 62.7 %collective-permute-start.8 = (bf16[272,2048]{1,0:T(8,128)(2,1)}, bf16[272,2048]{1,0:T(8,128)(2,1)}, u32[]{:S(2)}, u32[]{:S(2)}) collective-permute-start(bf16[272,2048]{1,0:T(8,128)(2,1)} %shard_map.49.token_ref), channel_id=1, source_target_pairs={{0,14},{1,15},{2,0},{3,1},{4,2},{5,3},{6,4},{7,5},{8,6},{9,7},{10,... | collective-permute-start | bytes 3342344 | tf_op jit(solution)/shard_map/ppermute | solution.py:237
  57.6 52.8 %collective-permute-start.9 = (bf16[272,2048]{1,0:T(8,128)(2,1)}, bf16[272,2048]{1,0:T(8,128)(2,1)}, u32[]{:S(2)}, u32[]{:S(2)}) collective-permute-start(bf16[272,2048]{1,0:T(8,128)(2,1)} %shard_map.50.token_ref.far_ref.far_tail), channel_id=1, source_target_pairs={{1,13},{3,15},{5,1},{7,3},{9,5},{11,7},{13,9},{15,11},{17,29},{19,... | collective-permute-start | bytes 3342344 | tf_op jit(solution)/shard_map/ppermute | solution.py:241
  95.4 24.5 %collective-permute-start.6 = (bf16[272,2048]{1,0:T(8,128)(2,1)}, bf16[272,2048]{1,0:T(8,128)(2,1)}, u32[]{:S(2)}, u32[]{:S(2)}) collective-permute-start(bf16[272,2048]{1,0:T(8,128)(2,1)} %shard_map.52), channel_id=1, source_target_pairs={{0,14},{1,15},{2,0},{3,1},{4,2},{5,3},{6,4},{7,5},{8,6},{9,7},{10,... | collective-permute-start | bytes 3342344 | tf_op jit(solution)/shard_map/ppermute | solution.py:237
  96.5 36.6 %collective-permute-start.7 = (bf16[272,2048]{1,0:T(8,128)(2,1)}, bf16[272,2048]{1,0:T(8,128)(2,1)}, u32[]{:S(2)}, u32[]{:S(2)}) collective-permute-start(bf16[272,2048]{1,0:T(8,128)(2,1)} %shard_map.51.token_ref.far_ref.far_tail), channel_id=1, source_target_pairs={{1,13},{3,15},{5,1},{7,3},{9,5},{11,7},{13,9},{15,11},{17,29},{19,... | collective-permute-start | bytes 3342344 | tf_op jit(solution)/shard_map/ppermute | solution.py:241

commit v3 on v2

--- a/solution.py
+++ b/solution.py
@@ -8,7 +8,6 @@
 from jax.sharding import PartitionSpec as P
 
 CHUNKS = 2
-ORDER = (("near", 0), ("far", 0), ("far", 1), ("near", 1))
 TILE = 256
 TAIL = 16
 BASE = 256
@@ -19,7 +18,7 @@
     return pl.CostEstimate(flops=flops, bytes_accessed=flops // 64, transcendentals=0)
 
 
-def pack_kernel(q_ref, picks_ref, out_ref):
+def pack_kernel(q_ref, picks_ref, token_ref, out_ref):
     steps, topk, rows = picks_ref.shape
     out_ref[:rows, :] = q_ref[...]
     out_ref[rows:, :] = jnp.zeros((TAIL, out_ref.shape[1]), out_ref.dtype)
@@ -29,7 +28,7 @@
         out_ref[rows:, s * rows : (s + 1) * rows] = jnp.concatenate(halves, axis=0).astype(out_ref.dtype)
 
 
-def pack(queries, picks, first, rows):
+def pack(queries, picks, token, first, rows):
     width = queries.shape[1]
     at = first // rows
     return pl.pallas_call(
@@ -39,11 +38,12 @@
         in_specs=[
             pl.BlockSpec((rows, width), lambda i: (at, 0)),
             pl.BlockSpec((*picks.shape[:2], rows), lambda i: (0, 0, at)),
+            pl.BlockSpec(memory_space=pl.ANY),
         ],
         out_specs=pl.BlockSpec((rows + TAIL, width), lambda i: (0, 0)),
         compiler_params=pltpu.CompilerParams(vmem_limit_bytes=VMEM_BYTES),
         cost_estimate=cost(rows * width),
-    )(queries, picks)
+    )(queries, picks, token)
 
 
 def unpack(tail, topk):
@@ -63,7 +63,19 @@
     return jnp.where(keep, picks, -1).T, (many * scale3).T
 
 
-def meet_kernel(n_src, gal_ids, scale3, topk, core_ref, live_ref, token_ref, *refs):
+def meet_kernel(active, n_token, *rest):
+    rest = rest[:7] + rest[6 + n_token :]
+    role = rest[4][1]
+    work = role == active[0]
+    for other in active[1:]:
+        work = work | (role == other)
+
+    @pl.when(work)
+    def _():
+        meet_work(*rest)
+
+
+def meet_work(n_src, gal_ids, scale3, topk, core_ref, live_ref, token_ref, *refs):
     n_gal = len(gal_ids)
     even = core_ref[0] == 0
     sources = [refs[i * (1 + 2 * n_gal) : (i + 1) * (1 + 2 * n_gal)] for i in range(n_src)]
@@ -119,7 +131,7 @@
     out_ref[rows:, :rows] = tail.astype(out_ref.dtype)
 
 
-def meet(core, lives, token, sources, gals, steps, rows, at, topk):
+def meet(core, lives, tokens, sources, gals, steps, rows, at, topk, active=(0, 1, 2)):
     gal_rows, width = gals[0].shape
     n_gal = len(gals)
     operands, specs = [], []
@@ -142,73 +154,105 @@
     if len(sources) == 2:
         scratch.append(pltpu.VMEM((rows, width), jnp.bfloat16))
     return pl.pallas_call(
-        functools.partial(meet_kernel, len(sources), tuple(s[0] for s in steps), float(width) ** -1.5, topk),
+        functools.partial(meet_kernel, active, len(tokens), len(sources), tuple(s[0] for s in steps), float(width) ** -1.5, topk),
         grid=(1,),
         out_shape=jax.ShapeDtypeStruct((rows + TAIL, width), jnp.bfloat16),
         in_specs=[
             pl.BlockSpec(memory_space=pltpu.SMEM),
             pl.BlockSpec(memory_space=pltpu.SMEM),
-            pl.BlockSpec(memory_space=pl.ANY),
         ]
+        + [pl.BlockSpec(memory_space=pl.ANY)] * len(tokens)
         + specs
         + [pl.BlockSpec((gal_rows, width), lambda i: (0, 0))] * n_gal,
         out_specs=pl.BlockSpec((rows + TAIL, width), lambda i: (0, 0)),
         scratch_shapes=scratch,
         compiler_params=pltpu.CompilerParams(vmem_limit_bytes=VMEM_BYTES),
         cost_estimate=cost(rows * width),
-    )(core, lives, token, *operands, *gals)
-
-
-def finish_kernel(core_ref, q_ref, own_ref, own_tail, near_ref, near_tail, far_ref, far_tail, back_ref, back_tail, *refs):
+    )(core, lives, *tokens, *operands, *gals)
+
+
+def after_kernel(x_ref, other_ref, out_ref):
+    pass
+
+
+def after(x, other):
+    return pl.pallas_call(
+        after_kernel,
+        out_shape=jax.ShapeDtypeStruct(x.shape, x.dtype),
+        in_specs=[pl.BlockSpec(memory_space=pl.ANY)] * 2,
+        out_specs=pl.BlockSpec(memory_space=pl.ANY),
+        input_output_aliases={0: 0},
+        compiler_params=pltpu.CompilerParams(vmem_limit_bytes=VMEM_BYTES),
+        cost_estimate=cost(1),
+    )(x, other)
+
+
+def gather_kernel(q_ref, own_ref, near_ref, token_ref, out_ref):
+    out_ref[...] = q_ref[...].astype(jnp.float32) + (own_ref[...].astype(jnp.float32) + near_ref[...].astype(jnp.float32))
+
+
+def gather(at, rows, queries, own, near, token, block=128):
+    width = queries.shape[1]
+    first = at * rows // block
+    here = pl.BlockSpec((block, width), lambda i: (first + i, 0))
+    alone = pl.BlockSpec((block, width), lambda i: (i, 0))
+    return pl.pallas_call(
+        gather_kernel,
+        grid=(rows // block,),
+        out_shape=jax.ShapeDtypeStruct((rows, width), jnp.float32),
+        in_specs=[here, here, alone, pl.BlockSpec(memory_space=pl.ANY)],
+        out_specs=alone,
+        compiler_params=pltpu.CompilerParams(vmem_limit_bytes=VMEM_BYTES),
+        cost_estimate=cost(64 * rows * width),
+    )(queries, own, near, token)
+
+
+def finish_kernel(block, flag_ref, sum_ref, own_tail, near_tail, *refs):
     out_ref = refs[-1]
-    rows = q_ref.shape[0]
-    even = core_ref[0] == 0
+    part = lax.rem(pl.program_id(0), 128 // block)
 
     def write(far_ref, far_tail):
         tails = own_tail[...].astype(jnp.float32) + near_tail[...].astype(jnp.float32) + far_tail[...].astype(jnp.float32)
-        mass = 1.0 + jnp.sum(tails.T, axis=1, keepdims=True)
-        total = own_ref[...].astype(jnp.float32) + near_ref[...].astype(jnp.float32) + far_ref[...].astype(jnp.float32)
-        out_ref[...] = ((q_ref[...].astype(jnp.float32) + total) / mass).astype(out_ref.dtype)
-
-    @pl.when(even)
-    def _():
-        write(far_ref, far_tail)
-
-    @pl.when(jnp.logical_not(even))
-    def _():
-        write(back_ref, back_tail)
-
-
-def finish(core, at, rows, queries, own, near, far, back, done, block=128):
-    width = queries.shape[1]
-    per = rows // block
-    first = at * per
-    operands, specs = [queries], [pl.BlockSpec((block, width), lambda i: (first + i, 0))]
-    for array, begin in ((own, first), (near, 0), (far, 0), (back, 0)):
-        tail_row = (array.shape[0] - TAIL) // TAIL
-        operands += [array, array]
-        specs.append(pl.BlockSpec((block, width), functools.partial(lambda o, i: (o + i, 0), begin)))
-        specs.append(pl.BlockSpec((TAIL, block), functools.partial(lambda t, o, i: (t, o + i), tail_row, begin)))
-    extra = {}
-    if done is not None:
-        operands.append(done)
-        specs.append(pl.BlockSpec(memory_space=pl.ANY))
-        extra = {"input_output_aliases": {len(operands): 0}}
-    return pl.pallas_call(
-        finish_kernel,
-        grid=(per,),
-        out_shape=jax.ShapeDtypeStruct(queries.shape, queries.dtype),
-        in_specs=[pl.BlockSpec(memory_space=pltpu.SMEM)] + specs,
+        share = 1.0 / (1.0 + jnp.sum(tails.T, axis=1, keepdims=True))
+        mine = share[:block]
+        for p in range(1, 128 // block):
+            mine = jnp.where(part == p, share[p * block : (p + 1) * block], mine)
+        out_ref[...] = ((sum_ref[...] + far_ref[...].astype(jnp.float32)) * mine).astype(out_ref.dtype)
+
+    for role in range(3):
+        pl.when(flag_ref[1] == role)(functools.partial(write, refs[2 * role], refs[2 * role + 1]))
+
+
+def finish(flags, at, rows, all_rows, sums, own, near, fars, done, block=128):
+    width = sums.shape[1]
+    first = at * rows // block
+    alone = pl.BlockSpec((block, width), lambda i: (i, 0))
+
+    def tail(array, begin):
+        row = (array.shape[0] - TAIL) // TAIL
+        return pl.BlockSpec((TAIL, 128), lambda i: (row, (begin + i) * block // 128))
+
+    operands = [flags, sums, own, near]
+    specs = [pl.BlockSpec(memory_space=pltpu.SMEM), alone, tail(own, first), tail(near, 0)]
+    for far in fars:
+        operands += [far, far]
+        specs += [alone, tail(far, 0)]
+    return pl.pallas_call(
+        functools.partial(finish_kernel, block),
+        grid=(rows // block,),
+        out_shape=jax.ShapeDtypeStruct((all_rows, width), jnp.bfloat16),
+        in_specs=specs + [pl.BlockSpec(memory_space=pl.ANY)],
         out_specs=pl.BlockSpec((block, width), lambda i: (first + i, 0)),
         compiler_params=pltpu.CompilerParams(vmem_limit_bytes=VMEM_BYTES),
-        cost_estimate=cost(rows * width),
-        **extra,
-    )(core, *operands)
+        cost_estimate=cost(64 * rows * width),
+        **({"input_output_aliases": {len(operands): 0}} if at > 0 else {}),
+    )(*operands, done)
 
 
 def on_device(queries, gallery, neighbors, counts):
     n = lax.axis_size("blk")
-    core = jnp.reshape(lax.axis_index("blk") % 2, (1,)).astype(jnp.int32)
+    me = lax.axis_index("blk").astype(jnp.int32)
+    core = jnp.stack([me % 2, (me % 2) * (1 + me % 4 // 2)])
     rows, width = queries.shape
     topk = neighbors.shape[2]
     picks = jnp.transpose(neighbors, (1, 2, 0))
@@ -216,32 +260,47 @@
     def shift(k):
         return [(i, (i + k) % n) for i in range(n)]
 
-    def odd_shift(k):
-        return [(i, (i + k) % n) for i in range(1, n, 2)]
+    def far_shift(k, *roles):
+        return [(i, (i + k) % n) for i in range(n) if i % 2 and 1 + i % 4 // 2 in roles]
 
     swap = [(i, i ^ 1) for i in range(n)]
 
     size = rows // CHUNKS
-    packed = [pack(queries, picks, c * size, size) for c in range(CHUNKS)]
+    packed = [pack(queries, picks, counts, c * size, size) for c in range(CHUNKS)]
+    early = lax.ppermute(packed[0], "blk", far_shift(4, 1))
     near = [lax.ppermute(chunk, "blk", shift(2)) for chunk in packed]
     other = lax.ppermute(gallery, "blk", swap)
     live = jnp.concatenate([counts, lax.ppermute(counts, "blk", swap)])
-    far = [lax.ppermute(chunk, "blk", odd_shift(4)) for chunk in packed]
-
-    own = meet(core, counts, packed[-1], [(queries, picks)], (gallery,), ((0, 0, 0),), rows, 0, topk)
+
+    token = packed[-1]
+    far_step = ((1, 1, 3),)
+    token = meet(core, live, [token], [packed[0], early], (other,), far_step, size, 0, topk, (0, 1))
+    far_here = [token]
+    early_back = lax.ppermute(token, "blk", far_shift(-4, 1))
+    late = []
+    for c in range(CHUNKS):
+        token = pack(queries, picks, token, c * size, size)
+        late.append(lax.ppermute(token, "blk", far_shift(4, 1, 2) if c else far_shift(4, 2)))
+    near_back = []
+    for c in range(CHUNKS):
+        token = meet(core, live, [token], [near[c]], (gallery, other), ((0, 2, 2), (1, 3, 1)), size, 0, topk)
+        token = after(token, near[-1]) if c + 1 < CHUNKS else token
+        near_back.append(lax.ppermute(token, "blk", shift(-2)))
+    token = meet(core, live, [token, early_back], [packed[0], late[0]], (other,), far_step, size, 0, topk, (2,))
+    fars = [(far_here[0], early_back, lax.ppermute(token, "blk", far_shift(-4, 2)))]
+    for c in range(1, CHUNKS):
+        token = meet(core, live, [token], [packed[c], late[c]], (other,), far_step, size, 0, topk)
+        back = lax.ppermute(token, "blk", far_shift(-4, 1, 2))
+        fars.append((token, back, back))
+    own = meet(core, counts, [token], [(queries, picks)], (gallery,), ((0, 0, 0),), rows, 0, topk)
     token = own
-    near_back, far_here, far_back = {}, {}, {}
-    for kind, c in ORDER:
-        if kind == "near":
-            token = meet(core, live, token, [near[c]], (gallery, other), ((0, 2, 2), (1, 3, 1)), size, 0, topk)
-            near_back[c] = lax.ppermute(token, "blk", shift(-2))
-        else:
-            token = meet(core, live, token, [packed[c], far[c]], (other,), ((1, 1, 3),), size, 0, topk)
-            far_here[c] = token
-            far_back[c] = lax.ppermute(token, "blk", odd_shift(-4))
-    done = None
+    sums, mark = [], token
     for c in range(CHUNKS):
-        done = finish(core, c, size, queries, own, near_back[c], far_here[c], far_back[c], done)
+        mark = gather(c, size, queries, own, near_back[c], mark)
+        sums.append(mark)
+    done = mark
+    for c in range(CHUNKS):
+        done = finish(core, c, size, rows, sums[c], own, near_back[c], fars[c], done)
     return done
 
 

time: 137 us -> 128 us (0.934)
  waiting for transfers between devices: 35.2 us -> 18.1 us
  Pallas kernels: 70.8 us -> 86.8 us
  starting transfers between devices: 28.9 us -> 20.6 us
    ppermute x2, waiting for transfers between devices: 14.9 us -> 2.54 us  [on_device(): near = [lax.ppermute(chunk, 'blk', shift(2)) for chunk in packed]]
    pallas_call x7 -> x11, Pallas kernels: 66.2 us -> 77.4 us  [the longest x6 64 us: meet(): pl.pallas_call(functools.partial(meet_kernel, active, len(tokens), len(so...]
    ppermute x6 -> x8, starting transfers between devices: 24.8 us -> 18 us  [the longest x1 4.64 us: on_device(): early = lax.ppermute(packed[0], 'blk', far_shift(4, 1))]
    pallas_call x2 -> x4, Pallas kernels: 4.62 us -> 9.33 us  [pack(): pl.pallas_call(pack_kernel, grid=(1,), out_shape=jax.ShapeDtypeStruct((ro...]
    ppermute x6 -> x8, waiting for transfers between devices: 19 us -> 15.5 us  [the longest x1 8.76 us: on_device(): early = lax.ppermute(packed[0], 'blk', far_shift(4, 1))]
    ppermute x2, starting transfers between devices: 3.93 us -> 2.52 us  [on_device(): near = [lax.ppermute(chunk, 'blk', shift(2)) for chunk in packed]]
  transfers between devices with their start and end apart: 10 -> 12, of which waited for: 5 -> 4; matrix products, arithmetic and copies ran while one was open for 1% -> 1% of each run, Pallas kernels for 49% -> 65%
where the time goes in v3:
time: 128 us
  Pallas kernels  86.8 us (68%)
  starting transfers between devices  20.6 us (16%)
  waiting for transfers between devices  18.1 us (14%)
  other arithmetic  1.84 us (1%)
    pallas_call x6, Pallas kernels, meet(): pl.pallas_call(functools.partial(meet_kernel, active, len(tokens), len(so...  64 us
    pallas_call x4, Pallas kernels, pack(): pl.pallas_call(pack_kernel, grid=(1,), out_shape=jax.ShapeDtypeStruct((ro...  9.33 us
    ppermute x1, waiting for transfers between devices, on_device(): early = lax.ppermute(packed[0], 'blk', far_shift(4, 1))  8.76 us
    pallas_call x2, Pallas kernels, finish(): pl.pallas_call(functools.partial(finish_kernel, block), grid=(rows // blo...  7.38 us
    pallas_call x2, Pallas kernels, gather(): pl.pallas_call(gather_kernel, grid=(rows // block,), out_shape=jax.ShapeD...  6.03 us
    ppermute x1, waiting for transfers between devices, on_device(): back = lax.ppermute(token, 'blk', far_shift(-4, 1, 2))  5.89 us
    ppermute x1, starting transfers between devices, on_device(): early = lax.ppermute(packed[0], 'blk', far_shift(4, 1))  4.64 us
    ppermute x2, starting transfers between devices, on_device(): lax.ppermute(token, 'blk', far_shift(4, 1, 2) if c else far_shift(4, 2))  3.55 us
  transfers between devices with their start and end apart: 12, of which 4 were waited for; matrix products, arithmetic and copies ran while one was open for 1% of the time, Pallas kernels for 65%

profile of v3, /device:TPU:1, one launch (start us, length us, event | category | flops | bytes accessed | tf_op | source)
XLA Modules:
  0.0 128.0 jit_solution(17222865770829716609)
XLA Ops:
  0.0 0.1 collective-permute-start.2
  0.7 2.4 %shard_map.47.rest_3_.rest_4_.rest_5_.rest_6_ = bf16[272,2048]{1,0:T(8,128)(2,1)} custom-call(bf16[512,2048]{1,0:T(8,128)(2,1)} %q_ref.11, s32[4,8,512]{2,1,0:T(8,128)} %bitcast.3, s32[1]{0:T(128)S(6)} %copy.9.token_ref.rest_1_), custom_call_target="tpu_custom_call" | custom-call | flops 524288 | bytes 8192 | tf_op jit(solution)/shard_map/pallas_call | solution.py:34
  3.1 4.6 %collective-permute-start.1 = (bf16[272,2048]{1,0:T(8,128)(2,1)}, bf16[272,2048]{1,0:T(8,128)(2,1)}, u32[]{:S(2)}, u32[]{:S(2)}) collective-permute-start(bf16[272,2048]{1,0:T(8,128)(2,1)} %shard_map.47.rest_3_.rest_4_.rest_5_.rest_6_), channel_id=1, source_target_pairs={{1,5},{5,9},{9,13},{13,1},{17,21},{21,25},{25,29},{29,17}} | collective-permute-start | bytes 3342344 | tf_op jit(solution)/shard_map/ppermute | solution.py:270
  7.7 0.1 collective-permute-start
  7.8 0.1 collective-permute-start.3
  7.9 2.3 %shard_map.46.rest_2_.rest_3_.rest_4_.rest_5_ = bf16[272,2048]{1,0:T(8,128)(2,1)} custom-call(bf16[512,2048]{1,0:T(8,128)(2,1)} %q_ref.11, s32[4,8,512]{2,1,0:T(8,128)} %bitcast.4, s32[1]{0:T(128)S(6)} %copy.9.token_ref.rest_1_), custom_call_target="tpu_custom_call" | custom-call | flops 524288 | bytes 8192 | tf_op jit(solution)/shard_map/pallas_call | solution.py:34
  10.2 2.5 %collective-permute-start.4 = (bf16[272,2048]{1,0:T(8,128)(2,1)}, bf16[272,2048]{1,0:T(8,128)(2,1)}, u32[]{:S(2)}, u32[]{:S(2)}) collective-permute-start(bf16[272,2048]{1,0:T(8,128)(2,1)} %shard_map.46.rest_2_.rest_3_.rest_4_.rest_5_), channel_id=1, source_target_pairs={{0,2},{1,3},{2,4},{3,5},{4,6},{5,7},{6,8},{7,9},{8,10},{9,11},{10,... | collective-permute-start | bytes 3342344 | tf_op jit(solution)/shard_map/ppermute | solution.py:271
  12.7 0.6 pad_add_fusion.rest_0_.flag_ref
  13.2 1.3 %pad_add_fusion.1.rest_1_ = s32[2]{0:T(128)} fusion(s32[1]{0:T(128)} %collective-permute-done, s32[1]{0:T(128)S(6)} %copy.9.token_ref.rest_1_), kind=kLoop, calls=%fused_computation.1 | loop fusion | flops 2 | bytes 16 | tf_op jit(solution)/shard_map/concatenate | solution.py:273
  14.5 8.8 %collective-permute-done.1.rest_6_.rest_7_.rest_8_ = bf16[272,2048]{1,0:T(8,128)(2,1)} collective-permute-done((bf16[272,2048]{1,0:T(8,128)(2,1)}, bf16[272,2048]{1,0:T(8,128)(2,1)}, u32[]{:S(2)}, u32[]{:S(2)}) %collective-permute-start.1) | collective-permute-done | bytes 1114144 | tf_op jit(solution)/shard_map/ppermute | solution.py:270
  23.3 8.7 %shard_map.48.token_ref.refs_0_.refs_1_ = bf16[272,2048]{1,0:T(8,128)(2,1)} custom-call(s32[2]{0:T(128)} %pad_add_fusion.rest_0_.flag_ref, s32[2]{0:T(128)} %pad_add_fusion.1.rest_1_, bf16[272,2048]{1,0:T(8,128)(2,1)} %shard_map.46.rest_2_.rest_3_.rest_4_.rest_5_, bf16[272,2048]{1,0:T(8,128)(2,1)} %shard_map.47.rest_3_.rest_4_.rest_5_.rest_6_, ...), custom_call_target="tpu_custom_call" | custom-call | flops 524288 | bytes 8192 | tf_op jit(solution)/shard_map/pallas_call | solution.py:156
  31.9 2.3 %shard_map.49.token_ref = bf16[272,2048]{1,0:T(8,128)(2,1)} custom-call(bf16[512,2048]{1,0:T(8,128)(2,1)} %q_ref.11, s32[4,8,512]{2,1,0:T(8,128)} %bitcast.5, bf16[272,2048]{1,0:T(8,128)(2,1)} %shard_map.48.token_ref.refs_0_.refs_1_), custom_call_target="tpu_custom_call" | custom-call | flops 524288 | bytes 8192 | tf_op jit(solution)/shard_map/pallas_call | solution.py:34
  34.2 1.6 %collective-permute-start.6 = (bf16[272,2048]{1,0:T(8,128)(2,1)}, bf16[272,2048]{1,0:T(8,128)(2,1)}, u32[]{:S(2)}, u32[]{:S(2)}) collective-permute-start(bf16[272,2048]{1,0:T(8,128)(2,1)} %shard_map.49.token_ref), channel_id=1, source_target_pairs={{3,7},{7,11},{11,15},{15,3},{19,23},{23,27},{27,31},{31,19}} | collective-permute-start | bytes 3342344 | tf_op jit(solution)/shard_map/ppermute | solution.py:283
  35.9 3.4 %collective-permute-start.5 = (bf16[272,2048]{1,0:T(8,128)(2,1)}, bf16[272,2048]{1,0:T(8,128)(2,1)}, u32[]{:S(2)}, u32[]{:S(2)}) collective-permute-start(bf16[272,2048]{1,0:T(8,128)(2,1)} %shard_map.48.token_ref.refs_0_.refs_1_), channel_id=1, source_target_pairs={{1,13},{5,1},{9,5},{13,9},{17,29},{21,17},{25,21},{29,25}} | collective-permute-start | bytes 3342344 | tf_op jit(solution)/shard_map/ppermute | solution.py:279
  39.3 2.3 %shard_map.50.rest_2_ = bf16[272,2048]{1,0:T(8,128)(2,1)} custom-call(bf16[512,2048]{1,0:T(8,128)(2,1)} %q_ref.11, s32[4,8,512]{2,1,0:T(8,128)} %bitcast.6, bf16[272,2048]{1,0:T(8,128)(2,1)} %shard_map.49.token_ref), custom_call_target="tpu_custom_call" | custom-call | flops 524288 | bytes 8192 | tf_op jit(solution)/shard_map/pallas_call | solution.py:34
  41.6 1.9 %collective-permute-start.7 = (bf16[272,2048]{1,0:T(8,128)(2,1)}, bf16[272,2048]{1,0:T(8,128)(2,1)}, u32[]{:S(2)}, u32[]{:S(2)}) collective-permute-start(bf16[272,2048]{1,0:T(8,128)(2,1)} %shard_map.50.rest_2_), channel_id=1, source_target_pairs={{1,5},{3,7},{5,9},{7,11},{9,13},{11,15},{13,1},{15,3},{17,21},{19,... | collective-permute-start | bytes 3342344 | tf_op jit(solution)/shard_map/ppermute | solution.py:283
  43.5 0.0 collective-permute-done.3.rest_3_.rest_4_.rest_5_.rest_6_.rest_7_
  43.5 14.4 %shard_map.51.x_ref = bf16[272,2048]{1,0:T(8,128)(2,1)} custom-call(s32[2]{0:T(128)} %pad_add_fusion.rest_0_.flag_ref, s32[2]{0:T(128)} %pad_add_fusion.1.rest_1_, bf16[272,2048]{1,0:T(8,128)(2,1)} %shard_map.50.rest_2_, bf16[272,2048]{1,0:T(8,128)(2,1)} %collective-permute-done.3.rest_3_.rest_4_.rest_5_.rest_6_.rest_7_, ...), custom_call_target="tpu_custom_call" | custom-call | flops 524288 | bytes 8192 | tf_op jit(solution)/shard_map/pallas_call | solution.py:156
  57.9 2.5 %collective-permute-done.4.other_ref.rest_3_.rest_4_.rest_5_.rest_6_.rest_7_ = bf16[272,2048]{1,0:T(8,128)(2,1)} collective-permute-done((bf16[272,2048]{1,0:T(8,128)(2,1)}, bf16[272,2048]{1,0:T(8,128)(2,1)}, u32[]{:S(2)}, u32[]{:S(2)}) %collective-permute-start.4) | collective-permute-done | bytes 1114144 | tf_op jit(solution)/shard_map/ppermute | solution.py:271
  60.5 14.4 %shard_map.53.rest_2_ = bf16[272,2048]{1,0:T(8,128)(2,1)} custom-call(s32[2]{0:T(128)} %pad_add_fusion.rest_0_.flag_ref, s32[2]{0:T(128)} %pad_add_fusion.1.rest_1_, bf16[272,2048]{1,0:T(8,128)(2,1)} %shard_map.52.rest_2_, bf16[272,2048]{1,0:T(8,128)(2,1)} %collective-permute-done.4.other_ref.rest_3_.rest_4_.rest_5_.rest_6_.rest_7_, ...), custom_call_target="tpu_custom_call" | custom-call | flops 524288 | bytes 8192 | tf_op jit(solution)/shard_map/pallas_call | solution.py:156
  74.9 1.9 %collective-permute-start.8 = (bf16[272,2048]{1,0:T(8,128)(2,1)}, bf16[272,2048]{1,0:T(8,128)(2,1)}, u32[]{:S(2)}, u32[]{:S(2)}) collective-permute-start(bf16[272,2048]{1,0:T(8,128)(2,1)} %shard_map.53.rest_2_), channel_id=1, source_target_pairs={{0,14},{1,15},{2,0},{3,1},{4,2},{5,3},{6,4},{7,5},{8,6},{9,7},{10,... | collective-permute-start | bytes 3342344 | tf_op jit(solution)/shard_map/ppermute | solution.py:288
  76.8 4.5 %shard_map.54.rest_2_ = bf16[272,2048]{1,0:T(8,128)(2,1)} custom-call(s32[2]{0:T(128)} %pad_add_fusion.rest_0_.flag_ref, s32[2]{0:T(128)} %pad_add_fusion.1.rest_1_, bf16[272,2048]{1,0:T(8,128)(2,1)} %shard_map.53.rest_2_, bf16[272,2048]{1,0:T(8,128)(2,1)} %collective-permute-done.5.rest_3_.refs_2_.refs_3_, ...), custom_call_target="tpu_custom_call" | custom-call | flops 524288 | bytes 8192 | tf_op jit(solution)/shard_map/pallas_call | solution.py:156
  81.3 1.6 %collective-permute-start.11 = (bf16[272,2048]{1,0:T(8,128)(2,1)}, bf16[272,2048]{1,0:T(8,128)(2,1)}, u32[]{:S(2)}, u32[]{:S(2)}) collective-permute-start(bf16[272,2048]{1,0:T(8,128)(2,1)} %shard_map.54.rest_2_), channel_id=1, source_target_pairs={{3,15},{7,3},{11,7},{15,11},{19,31},{23,19},{27,23},{31,27}} | collective-permute-start | bytes 3342344 | tf_op jit(solution)/shard_map/ppermute | solution.py:290
  83.0 9.0 %shard_map.55.rest_2_.refs_0_.refs_1_ = bf16[272,2048]{1,0:T(8,128)(2,1)} custom-call(s32[2]{0:T(128)} %pad_add_fusion.rest_0_.flag_ref, s32[2]{0:T(128)} %pad_add_fusion.1.rest_1_, bf16[272,2048]{1,0:T(8,128)(2,1)} %shard_map.54.rest_2_, bf16[272,2048]{1,0:T(8,128)(2,1)} %shard_map.46.rest_2_.rest_3_.rest_4_.rest_5_, ...), custom_call_target="tpu_custom_call" | custom-call | flops 524288 | bytes 8192 | tf_op jit(solution)/shard_map/pallas_call | solution.py:156
  92.0 2.9 %collective-permute-start.10 = (bf16[272,2048]{1,0:T(8,128)(2,1)}, bf16[272,2048]{1,0:T(8,128)(2,1)}, u32[]{:S(2)}, u32[]{:S(2)}) collective-permute-start(bf16[272,2048]{1,0:T(8,128)(2,1)} %shard_map.55.rest_2_.refs_0_.refs_1_), channel_id=1, source_target_pairs={{1,13},{3,15},{5,1},{7,3},{9,5},{11,7},{13,9},{15,11},{17,29},{19,... | collective-permute-start | bytes 3342344 | tf_op jit(solution)/shard_map/ppermute | solution.py:293
  94.8 13.0 %shard_map.56.own_ref.token_ref.own_tail = bf16[528,2048]{1,0:T(8,128)(2,1)} custom-call(s32[2]{0:T(128)} %pad_add_fusion.rest_0_.flag_ref, s32[1]{0:T(128)S(6)} %copy.9.token_ref.rest_1_, bf16[272,2048]{1,0:T(8,128)(2,1)} %shard_map.55.rest_2_.refs_0_.refs_1_, bf16[512,2048]{1,0:T(8,128)(2,1)} %q_ref.11, s32[4,8,512]{2,1,0:T(8,128)} %bitcast.7, ...), custom_call_target="tpu_custom_call" | custom-call | flops 1048576 | bytes 16384 | tf_op jit(solution)/shard_map/pallas_call | solution.py:156
  107.8 3.0 %shard_map.57.token_ref.sum_ref = f32[256,2048]{1,0:T(8,128)} custom-call(bf16[512,2048]{1,0:T(8,128)(2,1)} %q_ref.11, bf16[528,2048]{1,0:T(8,128)(2,1)} %shard_map.56.own_ref.token_ref.own_tail, bf16[272,2048]{1,0:T(8,128)(2,1)} %collective-permute-done.9.near_ref.near_tail, bf16[528,2048]{1,0:T(8,128)(2,1)} %shard_map.56.own_ref.token_ref.own_tail), custom_call_target="tpu_custom_call" | custom-call | flops 33554432 | bytes 524288 | tf_op jit(solution)/shard_map/pallas_call | solution.py:199
  110.9 0.9 collective-permute-done.8.near_ref.near_tail
  111.7 3.0 %shard_map.58.refs_6_.sum_ref = f32[256,2048]{1,0:T(8,128)} custom-call(bf16[512,2048]{1,0:T(8,128)(2,1)} %q_ref.11, bf16[528,2048]{1,0:T(8,128)(2,1)} %shard_map.56.own_ref.token_ref.own_tail, bf16[272,2048]{1,0:T(8,128)(2,1)} %collective-permute-done.8.near_ref.near_tail, f32[256,2048]{1,0:T(8,128)} %shard_map.57.token_ref.sum_ref), custom_call_target="tpu_custom_call" | custom-call | flops 33554432 | bytes 524288 | tf_op jit(solution)/shard_map/pallas_call | solution.py:199
  114.7 3.6 %shard_map.59.refs_6_ = bf16[512,2048]{1,0:T(8,128)(2,1)} custom-call(s32[2]{0:T(128)} %pad_add_fusion.rest_0_.flag_ref, f32[256,2048]{1,0:T(8,128)} %shard_map.57.token_ref.sum_ref, bf16[528,2048]{1,0:T(8,128)(2,1)} %shard_map.56.own_ref.token_ref.own_tail, bf16[272,2048]{1,0:T(8,128)(2,1)} %collective-permute-done.9.near_ref.near_tail, ...), custom_call_target="tpu_custom_call" | custom-call | flops 33554432 | bytes 524288 | tf_op jit(solution)/shard_map/pallas_call | solution.py:240
  118.3 5.9 %collective-permute-done.10.refs_2_.refs_3_.refs_4_.refs_5_ = bf16[272,2048]{1,0:T(8,128)(2,1)} collective-permute-done((bf16[272,2048]{1,0:T(8,128)(2,1)}, bf16[272,2048]{1,0:T(8,128)(2,1)}, u32[]{:S(2)}, u32[]{:S(2)}) %collective-permute-start.10) | collective-permute-done | bytes 1114144 | tf_op jit(solution)/shard_map/ppermute | solution.py:293
  124.2 3.8 %shard_map.60 = bf16[512,2048]{1,0:T(8,128)(2,1)} custom-call(s32[2]{0:T(128)} %pad_add_fusion.rest_0_.flag_ref, f32[256,2048]{1,0:T(8,128)} %shard_map.58.refs_6_.sum_ref, bf16[528,2048]{1,0:T(8,128)(2,1)} %shard_map.56.own_ref.token_ref.own_tail, bf16[272,2048]{1,0:T(8,128)(2,1)} %collective-permute-done.8.near_ref.near_tail, ...), custom_call_target="tpu_custom_call", output_to_operand_aliasing={{}: (10, {})} | custom-call | flops 33554432 | bytes 524288 | tf_op jit(solution)/shard_map/pallas_call | solution.py:240
  (9 shorter events, 0.0 us)
Async XLA Ops:
  0.0 23.3 %collective-permute-start.2 = (bf16[1536,2048]{1,0:T(8,128)(2,1)}, bf16[1536,2048]{1,0:T(8,128)(2,1)}, u32[]{:S(2)}, u32[]{:S(2)}) collective-permute-start(bf16[1536,2048]{1,0:T(8,128)(2,1)} %rest_6_.1), channel_id=1, source_target_pairs={{0,1},{1,0},{2,3},{3,2},{4,5},{5,4},{6,7},{7,6},{8,9},{9,8},{10,11... | collective-permute-start | bytes 18874376 | tf_op jit(solution)/shard_map/ppermute | solution.py:272
  3.1 20.2 %collective-permute-start.1 = (bf16[272,2048]{1,0:T(8,128)(2,1)}, bf16[272,2048]{1,0:T(8,128)(2,1)}, u32[]{:S(2)}, u32[]{:S(2)}) collective-permute-start(bf16[272,2048]{1,0:T(8,128)(2,1)} %shard_map.47.rest_3_.rest_4_.rest_5_.rest_6_), channel_id=1, source_target_pairs={{1,5},{5,9},{9,13},{13,1},{17,21},{21,25},{25,29},{29,17}} | collective-permute-start | bytes 3342344 | tf_op jit(solution)/shard_map/ppermute | solution.py:270
  7.7 5.5 %collective-permute-start = (s32[1]{0:T(128)}, s32[1]{0:T(128)}, u32[]{:S(2)}, u32[]{:S(2)}) collective-permute-start(s32[1]{0:T(128)} %param.7), channel_id=1, source_target_pairs={{0,1},{1,0},{2,3},{3,2},{4,5},{5,4},{6,7},{7,6},{8,9},{9,8},{10,11... | collective-permute-start | bytes 20 | tf_op jit(solution)/shard_map/ppermute | solution.py:273
  7.8 35.7 %collective-permute-start.3 = (bf16[272,2048]{1,0:T(8,128)(2,1)}, bf16[272,2048]{1,0:T(8,128)(2,1)}, u32[]{:S(2)}, u32[]{:S(2)}) collective-permute-start(bf16[272,2048]{1,0:T(8,128)(2,1)} %shard_map.47.rest_3_.rest_4_.rest_5_.rest_6_), channel_id=1, source_target_pairs={{0,2},{1,3},{2,4},{3,5},{4,6},{5,7},{6,8},{7,9},{8,10},{9,11},{10,... | collective-permute-start | bytes 3342344 | tf_op jit(solution)/shard_map/ppermute | solution.py:271
  10.2 50.3 %collective-permute-start.4 = (bf16[272,2048]{1,0:T(8,128)(2,1)}, bf16[272,2048]{1,0:T(8,128)(2,1)}, u32[]{:S(2)}, u32[]{:S(2)}) collective-permute-start(bf16[272,2048]{1,0:T(8,128)(2,1)} %shard_map.46.rest_2_.rest_3_.rest_4_.rest_5_), channel_id=1, source_target_pairs={{0,2},{1,3},{2,4},{3,5},{4,6},{5,7},{6,8},{7,9},{8,10},{9,11},{10,... | collective-permute-start | bytes 3342344 | tf_op jit(solution)/shard_map/ppermute | solution.py:271
  34.2 42.5 %collective-permute-start.6 = (bf16[272,2048]{1,0:T(8,128)(2,1)}, bf16[272,2048]{1,0:T(8,128)(2,1)}, u32[]{:S(2)}, u32[]{:S(2)}) collective-permute-start(bf16[272,2048]{1,0:T(8,128)(2,1)} %shard_map.49.token_ref), channel_id=1, source_target_pairs={{3,7},{7,11},{11,15},{15,3},{19,23},{23,27},{27,31},{31,19}} | collective-permute-start | bytes 3342344 | tf_op jit(solution)/shard_map/ppermute | solution.py:283
  35.9 40.9 %collective-permute-start.5 = (bf16[272,2048]{1,0:T(8,128)(2,1)}, bf16[272,2048]{1,0:T(8,128)(2,1)}, u32[]{:S(2)}, u32[]{:S(2)}) collective-permute-start(bf16[272,2048]{1,0:T(8,128)(2,1)} %shard_map.48.token_ref.refs_0_.refs_1_), channel_id=1, source_target_pairs={{1,13},{5,1},{9,5},{13,9},{17,29},{21,17},{25,21},{29,25}} | collective-permute-start | bytes 3342344 | tf_op jit(solution)/shard_map/ppermute | solution.py:279
  41.6 41.4 %collective-permute-start.7 = (bf16[272,2048]{1,0:T(8,128)(2,1)}, bf16[272,2048]{1,0:T(8,128)(2,1)}, u32[]{:S(2)}, u32[]{:S(2)}) collective-permute-start(bf16[272,2048]{1,0:T(8,128)(2,1)} %shard_map.50.rest_2_), channel_id=1, source_target_pairs={{1,5},{3,7},{5,9},{7,11},{9,13},{11,15},{13,1},{15,3},{17,21},{19,... | collective-permute-start | bytes 3342344 | tf_op jit(solution)/shard_map/ppermute | solution.py:283
  60.5 47.4 %collective-permute-start.9 = (bf16[272,2048]{1,0:T(8,128)(2,1)}, bf16[272,2048]{1,0:T(8,128)(2,1)}, u32[]{:S(2)}, u32[]{:S(2)}) collective-permute-start(bf16[272,2048]{1,0:T(8,128)(2,1)} %shard_map.52.rest_2_), channel_id=1, source_target_pairs={{0,14},{1,15},{2,0},{3,1},{4,2},{5,3},{6,4},{7,5},{8,6},{9,7},{10,... | collective-permute-start | bytes 3342344 | tf_op jit(solution)/shard_map/ppermute | solution.py:288
  74.9 36.9 %collective-permute-start.8 = (bf16[272,2048]{1,0:T(8,128)(2,1)}, bf16[272,2048]{1,0:T(8,128)(2,1)}, u32[]{:S(2)}, u32[]{:S(2)}) collective-permute-start(bf16[272,2048]{1,0:T(8,128)(2,1)} %shard_map.53.rest_2_), channel_id=1, source_target_pairs={{0,14},{1,15},{2,0},{3,1},{4,2},{5,3},{6,4},{7,5},{8,6},{9,7},{10,... | collective-permute-start | bytes 3342344 | tf_op jit(solution)/shard_map/ppermute | solution.py:288
  81.3 33.4 %collective-permute-start.11 = (bf16[272,2048]{1,0:T(8,128)(2,1)}, bf16[272,2048]{1,0:T(8,128)(2,1)}, u32[]{:S(2)}, u32[]{:S(2)}) collective-permute-start(bf16[272,2048]{1,0:T(8,128)(2,1)} %shard_map.54.rest_2_), channel_id=1, source_target_pairs={{3,15},{7,3},{11,7},{15,11},{19,31},{23,19},{27,23},{31,27}} | collective-permute-start | bytes 3342344 | tf_op jit(solution)/shard_map/ppermute | solution.py:290
  92.0 32.3 %collective-permute-start.10 = (bf16[272,2048]{1,0:T(8,128)(2,1)}, bf16[272,2048]{1,0:T(8,128)(2,1)}, u32[]{:S(2)}, u32[]{:S(2)}) collective-permute-start(bf16[272,2048]{1,0:T(8,128)(2,1)} %shard_map.55.rest_2_.refs_0_.refs_1_), channel_id=1, source_target_pairs={{1,13},{3,15},{5,1},{7,3},{9,5},{11,7},{13,9},{15,11},{17,29},{19,... | collective-permute-start | bytes 3342344 | tf_op jit(solution)/shard_map/ppermute | solution.py:293

commit v4 on v3

--- a/solution.py
+++ b/solution.py
@@ -63,7 +63,7 @@
     return jnp.where(keep, picks, -1).T, (many * scale3).T
 
 
-def meet_kernel(active, n_token, *rest):
+def meet_kernel(active, n_token, carry, *rest):
     rest = rest[:7] + rest[6 + n_token :]
     role = rest[4][1]
     work = role == active[0]
@@ -72,20 +72,26 @@
 
     @pl.when(work)
     def _():
-        meet_work(*rest)
-
-
-def meet_work(n_src, gal_ids, scale3, topk, core_ref, live_ref, token_ref, *refs):
+        meet_work(carry, *rest)
+
+
+def meet_work(carry, n_src, gal_ids, scale3, topk, core_ref, live_ref, token_ref, *refs):
     n_gal = len(gal_ids)
     even = core_ref[0] == 0
     sources = [refs[i * (1 + 2 * n_gal) : (i + 1) * (1 + 2 * n_gal)] for i in range(n_src)]
     refs = refs[n_src * (1 + 2 * n_gal) :]
     gal_refs, refs = refs[:n_gal], refs[n_gal:]
-    out_ref, w_ref = refs[:2]
+    before_ref = tail_ref = None
+    if carry == "in":
+        before_ref, *refs = refs
+    out_ref, *refs = refs
+    if carry == "out":
+        tail_ref, *refs = refs
+    w_ref, *refs = refs
     q_ref = sources[0][0]
     rows = q_ref.shape[0]
     if n_src == 2:
-        far_ref, q_ref = sources[1][0], refs[2]
+        far_ref, q_ref = sources[1][0], refs[0]
 
         @pl.when(even)
         def _():
@@ -127,11 +133,19 @@
     mid = (mass - high).astype(jnp.bfloat16).astype(jnp.float32)
     part = lax.broadcasted_iota(jnp.int32, (TAIL, rows), 0)
     tail = jnp.where(part == 0, high, jnp.where(part == 1, mid, jnp.where(part == 2, mass - high - mid, 0.0)))
+    tail = tail.astype(out_ref.dtype)
+    if tail_ref is not None:
+        tail_ref[...] = tail
+        return
     out_ref[rows:, :] = jnp.zeros((TAIL, width), out_ref.dtype)
-    out_ref[rows:, :rows] = tail.astype(out_ref.dtype)
-
-
-def meet(core, lives, tokens, sources, gals, steps, rows, at, topk, active=(0, 1, 2)):
+    begin = 0
+    if before_ref is not None:
+        begin = before_ref.shape[1]
+        out_ref[rows:, :begin] = before_ref[...]
+    out_ref[rows:, begin : begin + rows] = tail
+
+
+def meet(core, lives, tokens, sources, gals, steps, rows, at, topk, active=(0, 1, 2), carry=None):
     gal_rows, width = gals[0].shape
     n_gal = len(gals)
     operands, specs = [], []
@@ -150,25 +164,35 @@
                     specs.append(
                         pl.BlockSpec((TAIL, rows), functools.partial(lambda s, i: (rows // TAIL, s), step))
                     )
+    mode = carry if carry is None or isinstance(carry, str) else "in"
+    extra, extra_specs = ([carry], [pl.BlockSpec(carry.shape, lambda i: (0, 0))]) if mode == "in" else ([], [])
+    high = rows + (0 if mode == "out" else TAIL)
+    out_shape = [jax.ShapeDtypeStruct((high, width), jnp.bfloat16)]
+    out_specs = [pl.BlockSpec((high, width), lambda i: (0, 0))]
+    if mode == "out":
+        out_shape.append(jax.ShapeDtypeStruct((TAIL, rows), jnp.bfloat16))
+        out_specs.append(pl.BlockSpec((TAIL, rows), lambda i: (0, 0)))
     scratch = [pltpu.VMEM((n_gal, rows, gal_rows), jnp.bfloat16)]
     if len(sources) == 2:
         scratch.append(pltpu.VMEM((rows, width), jnp.bfloat16))
-    return pl.pallas_call(
-        functools.partial(meet_kernel, active, len(tokens), len(sources), tuple(s[0] for s in steps), float(width) ** -1.5, topk),
+    results = pl.pallas_call(
+        functools.partial(meet_kernel, active, len(tokens), mode, len(sources), tuple(s[0] for s in steps), float(width) ** -1.5, topk),
         grid=(1,),
-        out_shape=jax.ShapeDtypeStruct((rows + TAIL, width), jnp.bfloat16),
+        out_shape=out_shape,
         in_specs=[
             pl.BlockSpec(memory_space=pltpu.SMEM),
             pl.BlockSpec(memory_space=pltpu.SMEM),
         ]
         + [pl.BlockSpec(memory_space=pl.ANY)] * len(tokens)
         + specs
-        + [pl.BlockSpec((gal_rows, width), lambda i: (0, 0))] * n_gal,
-        out_specs=pl.BlockSpec((rows + TAIL, width), lambda i: (0, 0)),
+        + [pl.BlockSpec((gal_rows, width), lambda i: (0, 0))] * n_gal
+        + extra_specs,
+        out_specs=out_specs,
         scratch_shapes=scratch,
         compiler_params=pltpu.CompilerParams(vmem_limit_bytes=VMEM_BYTES),
         cost_estimate=cost(rows * width),
-    )(core, lives, *tokens, *operands, *gals)
+    )(core, lives, *tokens, *operands, *gals, *extra)
+    return results if mode == "out" else results[0]
 
 
 def after_kernel(x_ref, other_ref, out_ref):
@@ -203,7 +227,7 @@
         in_specs=[here, here, alone, pl.BlockSpec(memory_space=pl.ANY)],
         out_specs=alone,
         compiler_params=pltpu.CompilerParams(vmem_limit_bytes=VMEM_BYTES),
-        cost_estimate=cost(64 * rows * width),
+        cost_estimate=cost(8192 * rows * width),
     )(queries, own, near, token)
 
 
@@ -233,7 +257,7 @@
         return pl.BlockSpec((TAIL, 128), lambda i: (row, (begin + i) * block // 128))
 
     operands = [flags, sums, own, near]
-    specs = [pl.BlockSpec(memory_space=pltpu.SMEM), alone, tail(own, first), tail(near, 0)]
+    specs = [pl.BlockSpec(memory_space=pltpu.SMEM), alone, tail(own, first), tail(near, first)]
     for far in fars:
         operands += [far, far]
         specs += [alone, tail(far, 0)]
@@ -281,11 +305,12 @@
     for c in range(CHUNKS):
         token = pack(queries, picks, token, c * size, size)
         late.append(lax.ppermute(token, "blk", far_shift(4, 1, 2) if c else far_shift(4, 2)))
-    near_back = []
-    for c in range(CHUNKS):
-        token = meet(core, live, [token], [near[c]], (gallery, other), ((0, 2, 2), (1, 3, 1)), size, 0, topk)
-        token = after(token, near[-1]) if c + 1 < CHUNKS else token
-        near_back.append(lax.ppermute(token, "blk", shift(-2)))
+    near_step = ((0, 2, 2), (1, 3, 1))
+    total, tail = meet(core, live, [token], [near[0]], (gallery, other), near_step, size, 0, topk, carry="out")
+    total = after(total, near[1])
+    near_back = [lax.ppermute(total, "blk", shift(-2))]
+    token = meet(core, live, [total], [near[1]], (gallery, other), near_step, size, 0, topk, carry=tail)
+    near_back.append(lax.ppermute(token, "blk", shift(-2)))
     token = meet(core, live, [token, early_back], [packed[0], late[0]], (other,), far_step, size, 0, topk, (2,))
     fars = [(far_here[0], early_back, lax.ppermute(token, "blk", far_shift(-4, 2)))]
     for c in range(1, CHUNKS):
@@ -300,7 +325,7 @@
         sums.append(mark)
     done = mark
     for c in range(CHUNKS):
-        done = finish(core, c, size, rows, sums[c], own, near_back[c], fars[c], done)
+        done = finish(core, c, size, rows, sums[c], own, near_back[-1], fars[c], done)
     return done
 
 

time: 128 us -> 127 us (level)
  waiting for transfers between devices: 18.1 us -> 16.4 us
  transfers between devices with their start and end apart: 12 -> 12, of which waited for: 4 -> 4; matrix products, arithmetic and copies ran while one was open for 1% -> 2% of each run, Pallas kernels for 65% -> 66%
where the time goes in v4:
time: 127 us
  Pallas kernels  86.8 us (68%)
  starting transfers between devices  20.7 us (16%)
  waiting for transfers between devices  16.4 us (13%)
  other arithmetic  1.92 us (2%)
    pallas_call x6, Pallas kernels, meet(): pl.pallas_call(functools.partial(meet_kernel, active, len(tokens), mode,...  64.1 us
    pallas_call x4, Pallas kernels, pack(): pl.pallas_call(pack_kernel, grid=(1,), out_shape=jax.ShapeDtypeStruct((ro...  9.34 us
    ppermute x1, waiting for transfers between devices, on_device(): early = lax.ppermute(packed[0], 'blk', far_shift(4, 1))  8.14 us
    pallas_call x2, Pallas kernels, finish(): pl.pallas_call(functools.partial(finish_kernel, block), grid=(rows // blo...  7.36 us
    pallas_call x2, Pallas kernels, gather(): pl.pallas_call(gather_kernel, grid=(rows // block,), out_shape=jax.ShapeD...  6.04 us
    ppermute x1, waiting for transfers between devices, on_device(): back = lax.ppermute(token, 'blk', far_shift(-4, 1, 2))  5.87 us
    ppermute x1, starting transfers between devices, on_device(): early = lax.ppermute(packed[0], 'blk', far_shift(4, 1))  4.64 us
    ppermute x2, starting transfers between devices, on_device(): lax.ppermute(token, 'blk', far_shift(4, 1, 2) if c else far_shift(4, 2))  3.56 us
  transfers between devices with their start and end apart: 12, of which 4 were waited for; matrix products, arithmetic and copies ran while one was open for 2% of the time, Pallas kernels for 66%

profile of v4, /device:TPU:1, one launch (start us, length us, event | category | flops | bytes accessed | tf_op | source)
XLA Modules:
  0.0 126.6 jit_solution(3345062669739991242)
XLA Ops:
  0.0 0.1 collective-permute-start.2
  0.7 2.4 %shard_map.47.rest_3_.rest_4_.rest_5_.rest_6_ = bf16[272,2048]{1,0:T(8,128)(2,1)} custom-call(bf16[512,2048]{1,0:T(8,128)(2,1)} %q_ref.11, s32[4,8,512]{2,1,0:T(8,128)} %bitcast.3, s32[1]{0:T(128)S(6)} %copy.9.token_ref.rest_1_), custom_call_target="tpu_custom_call" | custom-call | flops 524288 | bytes 8192 | tf_op jit(solution)/shard_map/pallas_call | solution.py:34
  3.1 4.6 %collective-permute-start.1 = (bf16[272,2048]{1,0:T(8,128)(2,1)}, bf16[272,2048]{1,0:T(8,128)(2,1)}, u32[]{:S(2)}, u32[]{:S(2)}) collective-permute-start(bf16[272,2048]{1,0:T(8,128)(2,1)} %shard_map.47.rest_3_.rest_4_.rest_5_.rest_6_), channel_id=1, source_target_pairs={{1,5},{5,9},{9,13},{13,1},{17,21},{21,25},{25,29},{29,17}} | collective-permute-start | bytes 3342344 | tf_op jit(solution)/shard_map/ppermute | solution.py:294
  7.8 0.1 collective-permute-start.3
  7.8 2.3 %shard_map.46.rest_2_.rest_3_.rest_4_.rest_5_ = bf16[272,2048]{1,0:T(8,128)(2,1)} custom-call(bf16[512,2048]{1,0:T(8,128)(2,1)} %q_ref.11, s32[4,8,512]{2,1,0:T(8,128)} %bitcast.4, s32[1]{0:T(128)S(6)} %copy.9.token_ref.rest_1_), custom_call_target="tpu_custom_call" | custom-call | flops 524288 | bytes 8192 | tf_op jit(solution)/shard_map/pallas_call | solution.py:34
  10.1 2.5 %collective-permute-start.4 = (bf16[272,2048]{1,0:T(8,128)(2,1)}, bf16[272,2048]{1,0:T(8,128)(2,1)}, u32[]{:S(2)}, u32[]{:S(2)}) collective-permute-start(bf16[272,2048]{1,0:T(8,128)(2,1)} %shard_map.46.rest_2_.rest_3_.rest_4_.rest_5_), channel_id=1, source_target_pairs={{0,2},{1,3},{2,4},{3,5},{4,6},{5,7},{6,8},{7,9},{8,10},{9,11},{10,... | collective-permute-start | bytes 3342344 | tf_op jit(solution)/shard_map/ppermute | solution.py:295
  12.6 0.0 collective-permute-start
  12.6 0.6 pad_add_fusion.rest_0_.flag_ref
  13.2 0.6 collective-permute-done
  13.8 1.3 %pad_add_fusion.1.rest_1_ = s32[2]{0:T(128)} fusion(s32[1]{0:T(128)} %collective-permute-done, s32[1]{0:T(128)S(6)} %copy.9.token_ref.rest_1_), kind=kLoop, calls=%fused_computation.1 | loop fusion | flops 2 | bytes 16 | tf_op jit(solution)/shard_map/concatenate | solution.py:297
  15.1 8.1 %collective-permute-done.1.rest_6_.rest_7_.rest_8_ = bf16[272,2048]{1,0:T(8,128)(2,1)} collective-permute-done((bf16[272,2048]{1,0:T(8,128)(2,1)}, bf16[272,2048]{1,0:T(8,128)(2,1)}, u32[]{:S(2)}, u32[]{:S(2)}) %collective-permute-start.1) | collective-permute-done | bytes 1114144 | tf_op jit(solution)/shard_map/ppermute | solution.py:294
  23.3 8.7 %shard_map.48.token_ref.refs_0_.refs_1_ = bf16[272,2048]{1,0:T(8,128)(2,1)} custom-call(s32[2]{0:T(128)} %pad_add_fusion.rest_0_.flag_ref, s32[2]{0:T(128)} %pad_add_fusion.1.rest_1_, bf16[272,2048]{1,0:T(8,128)(2,1)} %shard_map.46.rest_2_.rest_3_.rest_4_.rest_5_, bf16[272,2048]{1,0:T(8,128)(2,1)} %shard_map.47.rest_3_.rest_4_.rest_5_.rest_6_, ...), custom_call_target="tpu_custom_call" | custom-call | flops 524288 | bytes 8192 | tf_op jit(solution)/shard_map/pallas_call | solution.py:178
  32.0 2.3 %shard_map.49.token_ref = bf16[272,2048]{1,0:T(8,128)(2,1)} custom-call(bf16[512,2048]{1,0:T(8,128)(2,1)} %q_ref.11, s32[4,8,512]{2,1,0:T(8,128)} %bitcast.5, bf16[272,2048]{1,0:T(8,128)(2,1)} %shard_map.48.token_ref.refs_0_.refs_1_), custom_call_target="tpu_custom_call" | custom-call | flops 524288 | bytes 8192 | tf_op jit(solution)/shard_map/pallas_call | solution.py:34
  34.3 1.6 %collective-permute-start.6 = (bf16[272,2048]{1,0:T(8,128)(2,1)}, bf16[272,2048]{1,0:T(8,128)(2,1)}, u32[]{:S(2)}, u32[]{:S(2)}) collective-permute-start(bf16[272,2048]{1,0:T(8,128)(2,1)} %shard_map.49.token_ref), channel_id=1, source_target_pairs={{3,7},{7,11},{11,15},{15,3},{19,23},{23,27},{27,31},{31,19}} | collective-permute-start | bytes 3342344 | tf_op jit(solution)/shard_map/ppermute | solution.py:307
  35.9 3.3 %collective-permute-start.5 = (bf16[272,2048]{1,0:T(8,128)(2,1)}, bf16[272,2048]{1,0:T(8,128)(2,1)}, u32[]{:S(2)}, u32[]{:S(2)}) collective-permute-start(bf16[272,2048]{1,0:T(8,128)(2,1)} %shard_map.48.token_ref.refs_0_.refs_1_), channel_id=1, source_target_pairs={{1,13},{5,1},{9,5},{13,9},{17,29},{21,17},{25,21},{29,25}} | collective-permute-start | bytes 3342344 | tf_op jit(solution)/shard_map/ppermute | solution.py:303
  39.3 2.3 %shard_map.50.rest_2_ = bf16[272,2048]{1,0:T(8,128)(2,1)} custom-call(bf16[512,2048]{1,0:T(8,128)(2,1)} %q_ref.11, s32[4,8,512]{2,1,0:T(8,128)} %bitcast.6, bf16[272,2048]{1,0:T(8,128)(2,1)} %shard_map.49.token_ref), custom_call_target="tpu_custom_call" | custom-call | flops 524288 | bytes 8192 | tf_op jit(solution)/shard_map/pallas_call | solution.py:34
  41.6 1.9 %collective-permute-start.7 = (bf16[272,2048]{1,0:T(8,128)(2,1)}, bf16[272,2048]{1,0:T(8,128)(2,1)}, u32[]{:S(2)}, u32[]{:S(2)}) collective-permute-start(bf16[272,2048]{1,0:T(8,128)(2,1)} %shard_map.50.rest_2_), channel_id=1, source_target_pairs={{1,5},{3,7},{5,9},{7,11},{9,13},{11,15},{13,1},{15,3},{17,21},{19,... | collective-permute-start | bytes 3342344 | tf_op jit(solution)/shard_map/ppermute | solution.py:307
  43.5 14.4 %shard_map.51 = (bf16[256,2048]{1,0:T(8,128)(2,1)}, bf16[16,256]{1,0:T(8,128)(2,1)}) custom-call(s32[2]{0:T(128)} %pad_add_fusion.rest_0_.flag_ref, s32[2]{0:T(128)} %pad_add_fusion.1.rest_1_, bf16[272,2048]{1,0:T(8,128)(2,1)} %shard_map.50.rest_2_, bf16[272,2048]{1,0:T(8,128)(2,1)} %collective-permute-done.3.rest_3_.rest_4_.rest_5_.rest_6_.rest_7_, ...), custom_call_target="tpu_custom_call" | custom-call | flops 524288 | bytes 8192 | tf_op jit(solution)/shard_map/pallas_call | solution.py:178
  58.0 1.8 %collective-permute-done.4.other_ref.rest_3_.rest_4_.rest_5_.rest_6_.rest_7_ = bf16[272,2048]{1,0:T(8,128)(2,1)} collective-permute-done((bf16[272,2048]{1,0:T(8,128)(2,1)}, bf16[272,2048]{1,0:T(8,128)(2,1)}, u32[]{:S(2)}, u32[]{:S(2)}) %collective-permute-start.4) | collective-permute-done | bytes 1114144 | tf_op jit(solution)/shard_map/ppermute | solution.py:295
  59.8 1.2 collective-permute-start.9
  60.9 14.4 %shard_map.53.rest_2_ = bf16[272,2048]{1,0:T(8,128)(2,1)} custom-call(s32[2]{0:T(128)} %pad_add_fusion.rest_0_.flag_ref, s32[2]{0:T(128)} %pad_add_fusion.1.rest_1_, bf16[256,2048]{1,0:T(8,128)(2,1)} %shard_map.52.rest_2_, bf16[272,2048]{1,0:T(8,128)(2,1)} %collective-permute-done.4.other_ref.rest_3_.rest_4_.rest_5_.rest_6_.rest_7_, ...), custom_call_target="tpu_custom_call" | custom-call | flops 524288 | bytes 8192 | tf_op jit(solution)/shard_map/pallas_call | solution.py:178
  75.3 1.6 %collective-permute-start.8 = (bf16[272,2048]{1,0:T(8,128)(2,1)}, bf16[272,2048]{1,0:T(8,128)(2,1)}, u32[]{:S(2)}, u32[]{:S(2)}) collective-permute-start(bf16[272,2048]{1,0:T(8,128)(2,1)} %shard_map.53.rest_2_), channel_id=1, source_target_pairs={{0,14},{1,15},{2,0},{3,1},{4,2},{5,3},{6,4},{7,5},{8,6},{9,7},{10,... | collective-permute-start | bytes 3342344 | tf_op jit(solution)/shard_map/ppermute | solution.py:313
  76.9 4.5 %shard_map.54.rest_2_ = bf16[272,2048]{1,0:T(8,128)(2,1)} custom-call(s32[2]{0:T(128)} %pad_add_fusion.rest_0_.flag_ref, s32[2]{0:T(128)} %pad_add_fusion.1.rest_1_, bf16[272,2048]{1,0:T(8,128)(2,1)} %shard_map.53.rest_2_, bf16[272,2048]{1,0:T(8,128)(2,1)} %collective-permute-done.5.rest_3_.refs_2_.refs_3_, ...), custom_call_target="tpu_custom_call" | custom-call | flops 524288 | bytes 8192 | tf_op jit(solution)/shard_map/pallas_call | solution.py:178
  81.4 1.6 %collective-permute-start.11 = (bf16[272,2048]{1,0:T(8,128)(2,1)}, bf16[272,2048]{1,0:T(8,128)(2,1)}, u32[]{:S(2)}, u32[]{:S(2)}) collective-permute-start(bf16[272,2048]{1,0:T(8,128)(2,1)} %shard_map.54.rest_2_), channel_id=1, source_target_pairs={{3,15},{7,3},{11,7},{15,11},{19,31},{23,19},{27,23},{31,27}} | collective-permute-start | bytes 3342344 | tf_op jit(solution)/shard_map/ppermute | solution.py:315
  83.1 9.0 %shard_map.55.rest_2_.refs_0_.refs_1_ = bf16[272,2048]{1,0:T(8,128)(2,1)} custom-call(s32[2]{0:T(128)} %pad_add_fusion.rest_0_.flag_ref, s32[2]{0:T(128)} %pad_add_fusion.1.rest_1_, bf16[272,2048]{1,0:T(8,128)(2,1)} %shard_map.54.rest_2_, bf16[272,2048]{1,0:T(8,128)(2,1)} %shard_map.46.rest_2_.rest_3_.rest_4_.rest_5_, ...), custom_call_target="tpu_custom_call" | custom-call | flops 524288 | bytes 8192 | tf_op jit(solution)/shard_map/pallas_call | solution.py:178
  92.1 2.2 %collective-permute-start.10 = (bf16[272,2048]{1,0:T(8,128)(2,1)}, bf16[272,2048]{1,0:T(8,128)(2,1)}, u32[]{:S(2)}, u32[]{:S(2)}) collective-permute-start(bf16[272,2048]{1,0:T(8,128)(2,1)} %shard_map.55.rest_2_.refs_0_.refs_1_), channel_id=1, source_target_pairs={{1,13},{3,15},{5,1},{7,3},{9,5},{11,7},{13,9},{15,11},{17,29},{19,... | collective-permute-start | bytes 3342344 | tf_op jit(solution)/shard_map/ppermute | solution.py:318
  94.3 13.0 %shard_map.56.own_ref.token_ref.own_tail = bf16[528,2048]{1,0:T(8,128)(2,1)} custom-call(s32[2]{0:T(128)} %pad_add_fusion.rest_0_.flag_ref, s32[1]{0:T(128)S(6)} %copy.9.token_ref.rest_1_, bf16[272,2048]{1,0:T(8,128)(2,1)} %shard_map.55.rest_2_.refs_0_.refs_1_, bf16[512,2048]{1,0:T(8,128)(2,1)} %q_ref.11, s32[4,8,512]{2,1,0:T(8,128)} %bitcast.7, ...), custom_call_target="tpu_custom_call" | custom-call | flops 1048576 | bytes 16384 | tf_op jit(solution)/shard_map/pallas_call | solution.py:178
  107.3 3.0 %shard_map.57.token_ref.sum_ref = f32[256,2048]{1,0:T(8,128)} custom-call(bf16[512,2048]{1,0:T(8,128)(2,1)} %q_ref.11, bf16[528,2048]{1,0:T(8,128)(2,1)} %shard_map.56.own_ref.token_ref.own_tail, bf16[256,2048]{1,0:T(8,128)(2,1)} %collective-permute-done.9.near_ref, bf16[528,2048]{1,0:T(8,128)(2,1)} %shard_map.56.own_ref.token_ref.own_tail), custom_call_target="tpu_custom_call" | custom-call | flops 4294967296 | bytes 67108864 | tf_op jit(solution)/shard_map/pallas_call | solution.py:223
  110.4 3.0 %shard_map.58.refs_6_.sum_ref = f32[256,2048]{1,0:T(8,128)} custom-call(bf16[512,2048]{1,0:T(8,128)(2,1)} %q_ref.11, bf16[528,2048]{1,0:T(8,128)(2,1)} %shard_map.56.own_ref.token_ref.own_tail, bf16[272,2048]{1,0:T(8,128)(2,1)} %collective-permute-done.8.near_ref.near_tail, f32[256,2048]{1,0:T(8,128)} %shard_map.57.token_ref.sum_ref), custom_call_target="tpu_custom_call" | custom-call | flops 4294967296 | bytes 67108864 | tf_op jit(solution)/shard_map/pallas_call | solution.py:223
  113.4 3.6 %shard_map.59.refs_6_ = bf16[512,2048]{1,0:T(8,128)(2,1)} custom-call(s32[2]{0:T(128)} %pad_add_fusion.rest_0_.flag_ref, f32[256,2048]{1,0:T(8,128)} %shard_map.57.token_ref.sum_ref, bf16[528,2048]{1,0:T(8,128)(2,1)} %shard_map.56.own_ref.token_ref.own_tail, bf16[272,2048]{1,0:T(8,128)(2,1)} %collective-permute-done.8.near_ref.near_tail, ...), custom_call_target="tpu_custom_call" | custom-call | flops 33554432 | bytes 524288 | tf_op jit(solution)/shard_map/pallas_call | solution.py:264
  117.0 5.9 %collective-permute-done.10.refs_2_.refs_3_.refs_4_.refs_5_ = bf16[272,2048]{1,0:T(8,128)(2,1)} collective-permute-done((bf16[272,2048]{1,0:T(8,128)(2,1)}, bf16[272,2048]{1,0:T(8,128)(2,1)}, u32[]{:S(2)}, u32[]{:S(2)}) %collective-permute-start.10) | collective-permute-done | bytes 1114144 | tf_op jit(solution)/shard_map/ppermute | solution.py:318
  122.9 3.8 %shard_map.60 = bf16[512,2048]{1,0:T(8,128)(2,1)} custom-call(s32[2]{0:T(128)} %pad_add_fusion.rest_0_.flag_ref, f32[256,2048]{1,0:T(8,128)} %shard_map.58.refs_6_.sum_ref, bf16[528,2048]{1,0:T(8,128)(2,1)} %shard_map.56.own_ref.token_ref.own_tail, bf16[272,2048]{1,0:T(8,128)(2,1)} %collective-permute-done.8.near_ref.near_tail, ...), custom_call_target="tpu_custom_call", output_to_operand_aliasing={{}: (10, {})} | custom-call | flops 33554432 | bytes 524288 | tf_op jit(solution)/shard_map/pallas_call | solution.py:264
  (9 shorter events, 0.0 us)
Async XLA Ops:
  0.0 23.3 %collective-permute-start.2 = (bf16[1536,2048]{1,0:T(8,128)(2,1)}, bf16[1536,2048]{1,0:T(8,128)(2,1)}, u32[]{:S(2)}, u32[]{:S(2)}) collective-permute-start(bf16[1536,2048]{1,0:T(8,128)(2,1)} %rest_6_.1), channel_id=1, source_target_pairs={{0,1},{1,0},{2,3},{3,2},{4,5},{5,4},{6,7},{7,6},{8,9},{9,8},{10,11... | collective-permute-start | bytes 18874376 | tf_op jit(solution)/shard_map/ppermute | solution.py:296
  3.1 20.2 %collective-permute-start.1 = (bf16[272,2048]{1,0:T(8,128)(2,1)}, bf16[272,2048]{1,0:T(8,128)(2,1)}, u32[]{:S(2)}, u32[]{:S(2)}) collective-permute-start(bf16[272,2048]{1,0:T(8,128)(2,1)} %shard_map.47.rest_3_.rest_4_.rest_5_.rest_6_), channel_id=1, source_target_pairs={{1,5},{5,9},{9,13},{13,1},{17,21},{21,25},{25,29},{29,17}} | collective-permute-start | bytes 3342344 | tf_op jit(solution)/shard_map/ppermute | solution.py:294
  7.8 35.8 %collective-permute-start.3 = (bf16[272,2048]{1,0:T(8,128)(2,1)}, bf16[272,2048]{1,0:T(8,128)(2,1)}, u32[]{:S(2)}, u32[]{:S(2)}) collective-permute-start(bf16[272,2048]{1,0:T(8,128)(2,1)} %shard_map.47.rest_3_.rest_4_.rest_5_.rest_6_), channel_id=1, source_target_pairs={{0,2},{1,3},{2,4},{3,5},{4,6},{5,7},{6,8},{7,9},{8,10},{9,11},{10,... | collective-permute-start | bytes 3342344 | tf_op jit(solution)/shard_map/ppermute | solution.py:295
  10.1 49.6 %collective-permute-start.4 = (bf16[272,2048]{1,0:T(8,128)(2,1)}, bf16[272,2048]{1,0:T(8,128)(2,1)}, u32[]{:S(2)}, u32[]{:S(2)}) collective-permute-start(bf16[272,2048]{1,0:T(8,128)(2,1)} %shard_map.46.rest_2_.rest_3_.rest_4_.rest_5_), channel_id=1, source_target_pairs={{0,2},{1,3},{2,4},{3,5},{4,6},{5,7},{6,8},{7,9},{8,10},{9,11},{10,... | collective-permute-start | bytes 3342344 | tf_op jit(solution)/shard_map/ppermute | solution.py:295
  12.6 1.2 collective-permute-start
  34.3 42.6 %collective-permute-start.6 = (bf16[272,2048]{1,0:T(8,128)(2,1)}, bf16[272,2048]{1,0:T(8,128)(2,1)}, u32[]{:S(2)}, u32[]{:S(2)}) collective-permute-start(bf16[272,2048]{1,0:T(8,128)(2,1)} %shard_map.49.token_ref), channel_id=1, source_target_pairs={{3,7},{7,11},{11,15},{15,3},{19,23},{23,27},{27,31},{31,19}} | collective-permute-start | bytes 3342344 | tf_op jit(solution)/shard_map/ppermute | solution.py:307
  35.9 41.0 %collective-permute-start.5 = (bf16[272,2048]{1,0:T(8,128)(2,1)}, bf16[272,2048]{1,0:T(8,128)(2,1)}, u32[]{:S(2)}, u32[]{:S(2)}) collective-permute-start(bf16[272,2048]{1,0:T(8,128)(2,1)} %shard_map.48.token_ref.refs_0_.refs_1_), channel_id=1, source_target_pairs={{1,13},{5,1},{9,5},{13,9},{17,29},{21,17},{25,21},{29,25}} | collective-permute-start | bytes 3342344 | tf_op jit(solution)/shard_map/ppermute | solution.py:303
  41.6 41.5 %collective-permute-start.7 = (bf16[272,2048]{1,0:T(8,128)(2,1)}, bf16[272,2048]{1,0:T(8,128)(2,1)}, u32[]{:S(2)}, u32[]{:S(2)}) collective-permute-start(bf16[272,2048]{1,0:T(8,128)(2,1)} %shard_map.50.rest_2_), channel_id=1, source_target_pairs={{1,5},{3,7},{5,9},{7,11},{9,13},{11,15},{13,1},{15,3},{17,21},{19,... | collective-permute-start | bytes 3342344 | tf_op jit(solution)/shard_map/ppermute | solution.py:307
  59.8 47.6 %collective-permute-start.9 = (bf16[256,2048]{1,0:T(8,128)(2,1)}, bf16[256,2048]{1,0:T(8,128)(2,1)}, u32[]{:S(2)}, u32[]{:S(2)}) collective-permute-start(bf16[256,2048]{1,0:T(8,128)(2,1)} %shard_map.52.rest_2_), channel_id=1, source_target_pairs={{0,14},{1,15},{2,0},{3,1},{4,2},{5,3},{6,4},{7,5},{8,6},{9,7},{10,... | collective-permute-start | bytes 3145736 | tf_op jit(solution)/shard_map/ppermute | solution.py:311
  75.3 35.0 %collective-permute-start.8 = (bf16[272,2048]{1,0:T(8,128)(2,1)}, bf16[272,2048]{1,0:T(8,128)(2,1)}, u32[]{:S(2)}, u32[]{:S(2)}) collective-permute-start(bf16[272,2048]{1,0:T(8,128)(2,1)} %shard_map.53.rest_2_), channel_id=1, source_target_pairs={{0,14},{1,15},{2,0},{3,1},{4,2},{5,3},{6,4},{7,5},{8,6},{9,7},{10,... | collective-permute-start | bytes 3342344 | tf_op jit(solution)/shard_map/ppermute | solution.py:313
  81.4 32.0 %collective-permute-start.11 = (bf16[272,2048]{1,0:T(8,128)(2,1)}, bf16[272,2048]{1,0:T(8,128)(2,1)}, u32[]{:S(2)}, u32[]{:S(2)}) collective-permute-start(bf16[272,2048]{1,0:T(8,128)(2,1)} %shard_map.54.rest_2_), channel_id=1, source_target_pairs={{3,15},{7,3},{11,7},{15,11},{19,31},{23,19},{27,23},{31,27}} | collective-permute-start | bytes 3342344 | tf_op jit(solution)/shard_map/ppermute | solution.py:315
  92.1 30.7 %collective-permute-start.10 = (bf16[272,2048]{1,0:T(8,128)(2,1)}, bf16[272,2048]{1,0:T(8,128)(2,1)}, u32[]{:S(2)}, u32[]{:S(2)}) collective-permute-start(bf16[272,2048]{1,0:T(8,128)(2,1)} %shard_map.55.rest_2_.refs_0_.refs_1_), channel_id=1, source_target_pairs={{1,13},{3,15},{5,1},{7,3},{9,5},{11,7},{13,9},{15,11},{17,29},{19,... | collective-permute-start | bytes 3342344 | tf_op jit(solution)/shard_map/ppermute | solution.py:318

commit v5 on v4

--- a/solution.py
+++ b/solution.py
@@ -231,7 +231,7 @@
     )(queries, own, near, token)
 
 
-def finish_kernel(block, flag_ref, sum_ref, own_tail, near_tail, *refs):
+def finish_kernel(block, sources, flag_ref, sum_ref, own_tail, near_tail, *refs):
     out_ref = refs[-1]
     part = lax.rem(pl.program_id(0), 128 // block)
 
@@ -244,7 +244,7 @@
         out_ref[...] = ((sum_ref[...] + far_ref[...].astype(jnp.float32)) * mine).astype(out_ref.dtype)
 
     for role in range(3):
-        pl.when(flag_ref[1] == role)(functools.partial(write, refs[2 * role], refs[2 * role + 1]))
+        pl.when(flag_ref[1] == role)(functools.partial(write, refs[2 * sources[role]], refs[2 * sources[role] + 1]))
 
 
 def finish(flags, at, rows, all_rows, sums, own, near, fars, done, block=128):
@@ -258,11 +258,13 @@
 
     operands = [flags, sums, own, near]
     specs = [pl.BlockSpec(memory_space=pltpu.SMEM), alone, tail(own, first), tail(near, first)]
-    for far in fars:
+    distinct = [far for i, far in enumerate(fars) if not any(far is other for other in fars[:i])]
+    sources = tuple(next(i for i, other in enumerate(distinct) if other is far) for far in fars)
+    for far in distinct:
         operands += [far, far]
         specs += [alone, tail(far, 0)]
     return pl.pallas_call(
-        functools.partial(finish_kernel, block),
+        functools.partial(finish_kernel, block, sources),
         grid=(rows // block,),
         out_shape=jax.ShapeDtypeStruct((all_rows, width), jnp.bfloat16),
         in_specs=specs + [pl.BlockSpec(memory_space=pl.ANY)],

time: 127 us -> 126 us (level)
  no operation moved by 1% of the time
where the time goes in v5:
time: 126 us
  Pallas kernels  86.3 us (68%)
  starting transfers between devices  20.7 us (16%)
  waiting for transfers between devices  16.4 us (13%)
  other arithmetic  1.92 us (2%)
    pallas_call x6, Pallas kernels, meet(): pl.pallas_call(functools.partial(meet_kernel, active, len(tokens), mode,...  64.1 us
    pallas_call x4, Pallas kernels, pack(): pl.pallas_call(pack_kernel, grid=(1,), out_shape=jax.ShapeDtypeStruct((ro...  9.34 us
    ppermute x1, waiting for transfers between devices, on_device(): early = lax.ppermute(packed[0], 'blk', far_shift(4, 1))  8.14 us
    pallas_call x2, Pallas kernels, finish(): pl.pallas_call(functools.partial(finish_kernel, block, sources), grid=(ro...  6.86 us
    pallas_call x2, Pallas kernels, gather(): pl.pallas_call(gather_kernel, grid=(rows // block,), out_shape=jax.ShapeD...  6.04 us
    ppermute x1, waiting for transfers between devices, on_device(): back = lax.ppermute(token, 'blk', far_shift(-4, 1, 2))  5.87 us
    ppermute x1, starting transfers between devices, on_device(): early = lax.ppermute(packed[0], 'blk', far_shift(4, 1))  4.64 us
    ppermute x2, starting transfers between devices, on_device(): lax.ppermute(token, 'blk', far_shift(4, 1, 2) if c else far_shift(4, 2))  3.56 us
  transfers between devices with their start and end apart: 12, of which 4 were waited for; matrix products, arithmetic and copies ran while one was open for 2% of the time, Pallas kernels for 66%

profile of v5, /device:TPU:1, one launch (start us, length us, event | category | flops | bytes accessed | tf_op | source)
XLA Modules:
  0.0 126.1 jit_solution(2732344933839555178)
XLA Ops:
  0.0 0.1 collective-permute-start.2
  0.7 2.4 %shard_map.47.rest_3_.rest_4_.rest_5_.rest_6_ = bf16[272,2048]{1,0:T(8,128)(2,1)} custom-call(bf16[512,2048]{1,0:T(8,128)(2,1)} %q_ref.11, s32[4,8,512]{2,1,0:T(8,128)} %bitcast.3, s32[1]{0:T(128)S(6)} %copy.9.token_ref.rest_1_), custom_call_target="tpu_custom_call" | custom-call | flops 524288 | bytes 8192 | tf_op jit(solution)/shard_map/pallas_call | solution.py:34
  3.1 4.6 %collective-permute-start.1 = (bf16[272,2048]{1,0:T(8,128)(2,1)}, bf16[272,2048]{1,0:T(8,128)(2,1)}, u32[]{:S(2)}, u32[]{:S(2)}) collective-permute-start(bf16[272,2048]{1,0:T(8,128)(2,1)} %shard_map.47.rest_3_.rest_4_.rest_5_.rest_6_), channel_id=1, source_target_pairs={{1,5},{5,9},{9,13},{13,1},{17,21},{21,25},{25,29},{29,17}} | collective-permute-start | bytes 3342344 | tf_op jit(solution)/shard_map/ppermute | solution.py:296
  7.8 0.1 collective-permute-start.3
  7.8 2.3 %shard_map.46.rest_2_.rest_3_.rest_4_.rest_5_ = bf16[272,2048]{1,0:T(8,128)(2,1)} custom-call(bf16[512,2048]{1,0:T(8,128)(2,1)} %q_ref.11, s32[4,8,512]{2,1,0:T(8,128)} %bitcast.4, s32[1]{0:T(128)S(6)} %copy.9.token_ref.rest_1_), custom_call_target="tpu_custom_call" | custom-call | flops 524288 | bytes 8192 | tf_op jit(solution)/shard_map/pallas_call | solution.py:34
  10.1 2.5 %collective-permute-start.4 = (bf16[272,2048]{1,0:T(8,128)(2,1)}, bf16[272,2048]{1,0:T(8,128)(2,1)}, u32[]{:S(2)}, u32[]{:S(2)}) collective-permute-start(bf16[272,2048]{1,0:T(8,128)(2,1)} %shard_map.46.rest_2_.rest_3_.rest_4_.rest_5_), channel_id=1, source_target_pairs={{0,2},{1,3},{2,4},{3,5},{4,6},{5,7},{6,8},{7,9},{8,10},{9,11},{10,... | collective-permute-start | bytes 3342344 | tf_op jit(solution)/shard_map/ppermute | solution.py:297
  12.6 0.0 collective-permute-start
  12.6 0.6 pad_add_fusion.rest_0_.flag_ref
  13.2 0.6 collective-permute-done
  13.8 1.3 %pad_add_fusion.1.rest_1_ = s32[2]{0:T(128)} fusion(s32[1]{0:T(128)} %collective-permute-done, s32[1]{0:T(128)S(6)} %copy.9.token_ref.rest_1_), kind=kLoop, calls=%fused_computation.1 | loop fusion | flops 2 | bytes 16 | tf_op jit(solution)/shard_map/concatenate | solution.py:299
  15.1 8.1 %collective-permute-done.1.rest_6_.rest_7_.rest_8_ = bf16[272,2048]{1,0:T(8,128)(2,1)} collective-permute-done((bf16[272,2048]{1,0:T(8,128)(2,1)}, bf16[272,2048]{1,0:T(8,128)(2,1)}, u32[]{:S(2)}, u32[]{:S(2)}) %collective-permute-start.1) | collective-permute-done | bytes 1114144 | tf_op jit(solution)/shard_map/ppermute | solution.py:296
  23.3 8.7 %shard_map.48.token_ref.refs_0_.refs_1_ = bf16[272,2048]{1,0:T(8,128)(2,1)} custom-call(s32[2]{0:T(128)} %pad_add_fusion.rest_0_.flag_ref, s32[2]{0:T(128)} %pad_add_fusion.1.rest_1_, bf16[272,2048]{1,0:T(8,128)(2,1)} %shard_map.46.rest_2_.rest_3_.rest_4_.rest_5_, bf16[272,2048]{1,0:T(8,128)(2,1)} %shard_map.47.rest_3_.rest_4_.rest_5_.rest_6_, ...), custom_call_target="tpu_custom_call" | custom-call | flops 524288 | bytes 8192 | tf_op jit(solution)/shard_map/pallas_call | solution.py:178
  32.0 2.3 %shard_map.49.token_ref = bf16[272,2048]{1,0:T(8,128)(2,1)} custom-call(bf16[512,2048]{1,0:T(8,128)(2,1)} %q_ref.11, s32[4,8,512]{2,1,0:T(8,128)} %bitcast.5, bf16[272,2048]{1,0:T(8,128)(2,1)} %shard_map.48.token_ref.refs_0_.refs_1_), custom_call_target="tpu_custom_call" | custom-call | flops 524288 | bytes 8192 | tf_op jit(solution)/shard_map/pallas_call | solution.py:34
  34.3 1.6 %collective-permute-start.6 = (bf16[272,2048]{1,0:T(8,128)(2,1)}, bf16[272,2048]{1,0:T(8,128)(2,1)}, u32[]{:S(2)}, u32[]{:S(2)}) collective-permute-start(bf16[272,2048]{1,0:T(8,128)(2,1)} %shard_map.49.token_ref), channel_id=1, source_target_pairs={{3,7},{7,11},{11,15},{15,3},{19,23},{23,27},{27,31},{31,19}} | collective-permute-start | bytes 3342344 | tf_op jit(solution)/shard_map/ppermute | solution.py:309
  35.9 3.3 %collective-permute-start.5 = (bf16[272,2048]{1,0:T(8,128)(2,1)}, bf16[272,2048]{1,0:T(8,128)(2,1)}, u32[]{:S(2)}, u32[]{:S(2)}) collective-permute-start(bf16[272,2048]{1,0:T(8,128)(2,1)} %shard_map.48.token_ref.refs_0_.refs_1_), channel_id=1, source_target_pairs={{1,13},{5,1},{9,5},{13,9},{17,29},{21,17},{25,21},{29,25}} | collective-permute-start | bytes 3342344 | tf_op jit(solution)/shard_map/ppermute | solution.py:305
  39.3 2.3 %shard_map.50.rest_2_ = bf16[272,2048]{1,0:T(8,128)(2,1)} custom-call(bf16[512,2048]{1,0:T(8,128)(2,1)} %q_ref.11, s32[4,8,512]{2,1,0:T(8,128)} %bitcast.6, bf16[272,2048]{1,0:T(8,128)(2,1)} %shard_map.49.token_ref), custom_call_target="tpu_custom_call" | custom-call | flops 524288 | bytes 8192 | tf_op jit(solution)/shard_map/pallas_call | solution.py:34
  41.6 1.9 %collective-permute-start.7 = (bf16[272,2048]{1,0:T(8,128)(2,1)}, bf16[272,2048]{1,0:T(8,128)(2,1)}, u32[]{:S(2)}, u32[]{:S(2)}) collective-permute-start(bf16[272,2048]{1,0:T(8,128)(2,1)} %shard_map.50.rest_2_), channel_id=1, source_target_pairs={{1,5},{3,7},{5,9},{7,11},{9,13},{11,15},{13,1},{15,3},{17,21},{19,... | collective-permute-start | bytes 3342344 | tf_op jit(solution)/shard_map/ppermute | solution.py:309
  43.5 14.4 %shard_map.51 = (bf16[256,2048]{1,0:T(8,128)(2,1)}, bf16[16,256]{1,0:T(8,128)(2,1)}) custom-call(s32[2]{0:T(128)} %pad_add_fusion.rest_0_.flag_ref, s32[2]{0:T(128)} %pad_add_fusion.1.rest_1_, bf16[272,2048]{1,0:T(8,128)(2,1)} %shard_map.50.rest_2_, bf16[272,2048]{1,0:T(8,128)(2,1)} %collective-permute-done.3.rest_3_.rest_4_.rest_5_.rest_6_.rest_7_, ...), custom_call_target="tpu_custom_call" | custom-call | flops 524288 | bytes 8192 | tf_op jit(solution)/shard_map/pallas_call | solution.py:178
  58.0 1.8 %collective-permute-done.4.other_ref.rest_3_.rest_4_.rest_5_.rest_6_.rest_7_ = bf16[272,2048]{1,0:T(8,128)(2,1)} collective-permute-done((bf16[272,2048]{1,0:T(8,128)(2,1)}, bf16[272,2048]{1,0:T(8,128)(2,1)}, u32[]{:S(2)}, u32[]{:S(2)}) %collective-permute-start.4) | collective-permute-done | bytes 1114144 | tf_op jit(solution)/shard_map/ppermute | solution.py:297
  59.8 1.2 collective-permute-start.9
  60.9 14.4 %shard_map.53.rest_2_ = bf16[272,2048]{1,0:T(8,128)(2,1)} custom-call(s32[2]{0:T(128)} %pad_add_fusion.rest_0_.flag_ref, s32[2]{0:T(128)} %pad_add_fusion.1.rest_1_, bf16[256,2048]{1,0:T(8,128)(2,1)} %shard_map.52.rest_2_, bf16[272,2048]{1,0:T(8,128)(2,1)} %collective-permute-done.4.other_ref.rest_3_.rest_4_.rest_5_.rest_6_.rest_7_, ...), custom_call_target="tpu_custom_call" | custom-call | flops 524288 | bytes 8192 | tf_op jit(solution)/shard_map/pallas_call | solution.py:178
  75.3 1.6 %collective-permute-start.8 = (bf16[272,2048]{1,0:T(8,128)(2,1)}, bf16[272,2048]{1,0:T(8,128)(2,1)}, u32[]{:S(2)}, u32[]{:S(2)}) collective-permute-start(bf16[272,2048]{1,0:T(8,128)(2,1)} %shard_map.53.rest_2_), channel_id=1, source_target_pairs={{0,14},{1,15},{2,0},{3,1},{4,2},{5,3},{6,4},{7,5},{8,6},{9,7},{10,... | collective-permute-start | bytes 3342344 | tf_op jit(solution)/shard_map/ppermute | solution.py:315
  76.9 4.5 %shard_map.54.rest_2_ = bf16[272,2048]{1,0:T(8,128)(2,1)} custom-call(s32[2]{0:T(128)} %pad_add_fusion.rest_0_.flag_ref, s32[2]{0:T(128)} %pad_add_fusion.1.rest_1_, bf16[272,2048]{1,0:T(8,128)(2,1)} %shard_map.53.rest_2_, bf16[272,2048]{1,0:T(8,128)(2,1)} %collective-permute-done.5.rest_3_.refs_2_.refs_3_, ...), custom_call_target="tpu_custom_call" | custom-call | flops 524288 | bytes 8192 | tf_op jit(solution)/shard_map/pallas_call | solution.py:178
  81.4 1.6 %collective-permute-start.11 = (bf16[272,2048]{1,0:T(8,128)(2,1)}, bf16[272,2048]{1,0:T(8,128)(2,1)}, u32[]{:S(2)}, u32[]{:S(2)}) collective-permute-start(bf16[272,2048]{1,0:T(8,128)(2,1)} %shard_map.54.rest_2_), channel_id=1, source_target_pairs={{3,15},{7,3},{11,7},{15,11},{19,31},{23,19},{27,23},{31,27}} | collective-permute-start | bytes 3342344 | tf_op jit(solution)/shard_map/ppermute | solution.py:317
  83.1 9.0 %shard_map.55.rest_2_.refs_0_.refs_1_ = bf16[272,2048]{1,0:T(8,128)(2,1)} custom-call(s32[2]{0:T(128)} %pad_add_fusion.rest_0_.flag_ref, s32[2]{0:T(128)} %pad_add_fusion.1.rest_1_, bf16[272,2048]{1,0:T(8,128)(2,1)} %shard_map.54.rest_2_, bf16[272,2048]{1,0:T(8,128)(2,1)} %shard_map.46.rest_2_.rest_3_.rest_4_.rest_5_, ...), custom_call_target="tpu_custom_call" | custom-call | flops 524288 | bytes 8192 | tf_op jit(solution)/shard_map/pallas_call | solution.py:178
  92.1 2.2 %collective-permute-start.10 = (bf16[272,2048]{1,0:T(8,128)(2,1)}, bf16[272,2048]{1,0:T(8,128)(2,1)}, u32[]{:S(2)}, u32[]{:S(2)}) collective-permute-start(bf16[272,2048]{1,0:T(8,128)(2,1)} %shard_map.55.rest_2_.refs_0_.refs_1_), channel_id=1, source_target_pairs={{1,13},{3,15},{5,1},{7,3},{9,5},{11,7},{13,9},{15,11},{17,29},{19,... | collective-permute-start | bytes 3342344 | tf_op jit(solution)/shard_map/ppermute | solution.py:320
  94.3 13.0 %shard_map.56.own_ref.token_ref.own_tail = bf16[528,2048]{1,0:T(8,128)(2,1)} custom-call(s32[2]{0:T(128)} %pad_add_fusion.rest_0_.flag_ref, s32[1]{0:T(128)S(6)} %copy.9.token_ref.rest_1_, bf16[272,2048]{1,0:T(8,128)(2,1)} %shard_map.55.rest_2_.refs_0_.refs_1_, bf16[512,2048]{1,0:T(8,128)(2,1)} %q_ref.11, s32[4,8,512]{2,1,0:T(8,128)} %bitcast.7, ...), custom_call_target="tpu_custom_call" | custom-call | flops 1048576 | bytes 16384 | tf_op jit(solution)/shard_map/pallas_call | solution.py:178
  107.3 3.0 %shard_map.57.token_ref.sum_ref = f32[256,2048]{1,0:T(8,128)} custom-call(bf16[512,2048]{1,0:T(8,128)(2,1)} %q_ref.11, bf16[528,2048]{1,0:T(8,128)(2,1)} %shard_map.56.own_ref.token_ref.own_tail, bf16[256,2048]{1,0:T(8,128)(2,1)} %collective-permute-done.9.near_ref, bf16[528,2048]{1,0:T(8,128)(2,1)} %shard_map.56.own_ref.token_ref.own_tail), custom_call_target="tpu_custom_call" | custom-call | flops 4294967296 | bytes 67108864 | tf_op jit(solution)/shard_map/pallas_call | solution.py:223
  110.4 3.0 %shard_map.58.refs_6_.sum_ref = f32[256,2048]{1,0:T(8,128)} custom-call(bf16[512,2048]{1,0:T(8,128)(2,1)} %q_ref.11, bf16[528,2048]{1,0:T(8,128)(2,1)} %shard_map.56.own_ref.token_ref.own_tail, bf16[272,2048]{1,0:T(8,128)(2,1)} %collective-permute-done.8.near_ref.near_tail, f32[256,2048]{1,0:T(8,128)} %shard_map.57.token_ref.sum_ref), custom_call_target="tpu_custom_call" | custom-call | flops 4294967296 | bytes 67108864 | tf_op jit(solution)/shard_map/pallas_call | solution.py:223
  113.4 3.6 %shard_map.59.refs_4_ = bf16[512,2048]{1,0:T(8,128)(2,1)} custom-call(s32[2]{0:T(128)} %pad_add_fusion.rest_0_.flag_ref, f32[256,2048]{1,0:T(8,128)} %shard_map.57.token_ref.sum_ref, bf16[528,2048]{1,0:T(8,128)(2,1)} %shard_map.56.own_ref.token_ref.own_tail, bf16[272,2048]{1,0:T(8,128)(2,1)} %collective-permute-done.8.near_ref.near_tail, ...), custom_call_target="tpu_custom_call" | custom-call | flops 33554432 | bytes 524288 | tf_op jit(solution)/shard_map/pallas_call | solution.py:266
  117.0 5.9 %collective-permute-done.10.refs_2_.refs_3_ = bf16[272,2048]{1,0:T(8,128)(2,1)} collective-permute-done((bf16[272,2048]{1,0:T(8,128)(2,1)}, bf16[272,2048]{1,0:T(8,128)(2,1)}, u32[]{:S(2)}, u32[]{:S(2)}) %collective-permute-start.10) | collective-permute-done | bytes 1114144 | tf_op jit(solution)/shard_map/ppermute | solution.py:320
  122.9 3.3 %shard_map.60 = bf16[512,2048]{1,0:T(8,128)(2,1)} custom-call(s32[2]{0:T(128)} %pad_add_fusion.rest_0_.flag_ref, f32[256,2048]{1,0:T(8,128)} %shard_map.58.refs_6_.sum_ref, bf16[528,2048]{1,0:T(8,128)(2,1)} %shard_map.56.own_ref.token_ref.own_tail, bf16[272,2048]{1,0:T(8,128)(2,1)} %collective-permute-done.8.near_ref.near_tail, ...), custom_call_target="tpu_custom_call", output_to_operand_aliasing={{}: (8, {})} | custom-call | flops 33554432 | bytes 524288 | tf_op jit(solution)/shard_map/pallas_call | solution.py:266
  (9 shorter events, 0.0 us)
Async XLA Ops:
  0.0 23.3 %collective-permute-start.2 = (bf16[1536,2048]{1,0:T(8,128)(2,1)}, bf16[1536,2048]{1,0:T(8,128)(2,1)}, u32[]{:S(2)}, u32[]{:S(2)}) collective-permute-start(bf16[1536,2048]{1,0:T(8,128)(2,1)} %rest_6_.1), channel_id=1, source_target_pairs={{0,1},{1,0},{2,3},{3,2},{4,5},{5,4},{6,7},{7,6},{8,9},{9,8},{10,11... | collective-permute-start | bytes 18874376 | tf_op jit(solution)/shard_map/ppermute | solution.py:298
  3.1 20.2 %collective-permute-start.1 = (bf16[272,2048]{1,0:T(8,128)(2,1)}, bf16[272,2048]{1,0:T(8,128)(2,1)}, u32[]{:S(2)}, u32[]{:S(2)}) collective-permute-start(bf16[272,2048]{1,0:T(8,128)(2,1)} %shard_map.47.rest_3_.rest_4_.rest_5_.rest_6_), channel_id=1, source_target_pairs={{1,5},{5,9},{9,13},{13,1},{17,21},{21,25},{25,29},{29,17}} | collective-permute-start | bytes 3342344 | tf_op jit(solution)/shard_map/ppermute | solution.py:296
  7.8 35.8 %collective-permute-start.3 = (bf16[272,2048]{1,0:T(8,128)(2,1)}, bf16[272,2048]{1,0:T(8,128)(2,1)}, u32[]{:S(2)}, u32[]{:S(2)}) collective-permute-start(bf16[272,2048]{1,0:T(8,128)(2,1)} %shard_map.47.rest_3_.rest_4_.rest_5_.rest_6_), channel_id=1, source_target_pairs={{0,2},{1,3},{2,4},{3,5},{4,6},{5,7},{6,8},{7,9},{8,10},{9,11},{10,... | collective-permute-start | bytes 3342344 | tf_op jit(solution)/shard_map/ppermute | solution.py:297
  10.1 49.6 %collective-permute-start.4 = (bf16[272,2048]{1,0:T(8,128)(2,1)}, bf16[272,2048]{1,0:T(8,128)(2,1)}, u32[]{:S(2)}, u32[]{:S(2)}) collective-permute-start(bf16[272,2048]{1,0:T(8,128)(2,1)} %shard_map.46.rest_2_.rest_3_.rest_4_.rest_5_), channel_id=1, source_target_pairs={{0,2},{1,3},{2,4},{3,5},{4,6},{5,7},{6,8},{7,9},{8,10},{9,11},{10,... | collective-permute-start | bytes 3342344 | tf_op jit(solution)/shard_map/ppermute | solution.py:297
  12.6 1.2 collective-permute-start
  34.3 42.6 %collective-permute-start.6 = (bf16[272,2048]{1,0:T(8,128)(2,1)}, bf16[272,2048]{1,0:T(8,128)(2,1)}, u32[]{:S(2)}, u32[]{:S(2)}) collective-permute-start(bf16[272,2048]{1,0:T(8,128)(2,1)} %shard_map.49.token_ref), channel_id=1, source_target_pairs={{3,7},{7,11},{11,15},{15,3},{19,23},{23,27},{27,31},{31,19}} | collective-permute-start | bytes 3342344 | tf_op jit(solution)/shard_map/ppermute | solution.py:309
  35.9 41.0 %collective-permute-start.5 = (bf16[272,2048]{1,0:T(8,128)(2,1)}, bf16[272,2048]{1,0:T(8,128)(2,1)}, u32[]{:S(2)}, u32[]{:S(2)}) collective-permute-start(bf16[272,2048]{1,0:T(8,128)(2,1)} %shard_map.48.token_ref.refs_0_.refs_1_), channel_id=1, source_target_pairs={{1,13},{5,1},{9,5},{13,9},{17,29},{21,17},{25,21},{29,25}} | collective-permute-start | bytes 3342344 | tf_op jit(solution)/shard_map/ppermute | solution.py:305
  41.6 41.5 %collective-permute-start.7 = (bf16[272,2048]{1,0:T(8,128)(2,1)}, bf16[272,2048]{1,0:T(8,128)(2,1)}, u32[]{:S(2)}, u32[]{:S(2)}) collective-permute-start(bf16[272,2048]{1,0:T(8,128)(2,1)} %shard_map.50.rest_2_), channel_id=1, source_target_pairs={{1,5},{3,7},{5,9},{7,11},{9,13},{11,15},{13,1},{15,3},{17,21},{19,... | collective-permute-start | bytes 3342344 | tf_op jit(solution)/shard_map/ppermute | solution.py:309
  59.8 47.6 %collective-permute-start.9 = (bf16[256,2048]{1,0:T(8,128)(2,1)}, bf16[256,2048]{1,0:T(8,128)(2,1)}, u32[]{:S(2)}, u32[]{:S(2)}) collective-permute-start(bf16[256,2048]{1,0:T(8,128)(2,1)} %shard_map.52.rest_2_), channel_id=1, source_target_pairs={{0,14},{1,15},{2,0},{3,1},{4,2},{5,3},{6,4},{7,5},{8,6},{9,7},{10,... | collective-permute-start | bytes 3145736 | tf_op jit(solution)/shard_map/ppermute | solution.py:313
  75.3 35.0 %collective-permute-start.8 = (bf16[272,2048]{1,0:T(8,128)(2,1)}, bf16[272,2048]{1,0:T(8,128)(2,1)}, u32[]{:S(2)}, u32[]{:S(2)}) collective-permute-start(bf16[272,2048]{1,0:T(8,128)(2,1)} %shard_map.53.rest_2_), channel_id=1, source_target_pairs={{0,14},{1,15},{2,0},{3,1},{4,2},{5,3},{6,4},{7,5},{8,6},{9,7},{10,... | collective-permute-start | bytes 3342344 | tf_op jit(solution)/shard_map/ppermute | solution.py:315
  81.4 32.0 %collective-permute-start.11 = (bf16[272,2048]{1,0:T(8,128)(2,1)}, bf16[272,2048]{1,0:T(8,128)(2,1)}, u32[]{:S(2)}, u32[]{:S(2)}) collective-permute-start(bf16[272,2048]{1,0:T(8,128)(2,1)} %shard_map.54.rest_2_), channel_id=1, source_target_pairs={{3,15},{7,3},{11,7},{15,11},{19,31},{23,19},{27,23},{31,27}} | collective-permute-start | bytes 3342344 | tf_op jit(solution)/shard_map/ppermute | solution.py:317
  92.1 30.7 %collective-permute-start.10 = (bf16[272,2048]{1,0:T(8,128)(2,1)}, bf16[272,2048]{1,0:T(8,128)(2,1)}, u32[]{:S(2)}, u32[]{:S(2)}) collective-permute-start(bf16[272,2048]{1,0:T(8,128)(2,1)} %shard_map.55.rest_2_.refs_0_.refs_1_), channel_id=1, source_target_pairs={{1,13},{3,15},{5,1},{7,3},{9,5},{11,7},{13,9},{15,11},{17,29},{19,... | collective-permute-start | bytes 3342344 | tf_op jit(solution)/shard_map/ppermute | solution.py:320
